TPU v7x, 128 devices: a whole 4x4x4 slice. The times are simulated.
128 devices in a mesh: dom: 32 (over z, x, core), hid: 4 (over y).
Axes of the slice: x: 4, y: 4, z: 4, core: 2. Of those that a mesh axis runs over, the one named last changes fastest.
Arguments:
- features: bfloat16 [393216, 512], P('dom', 'hid'), may hold values from -6 to 6
- neigh_mean: bfloat16 [393216, 512], P('dom', 'hid'), may hold values from -6 to 6
- pre_relu: bfloat16 [393216, 512], P('dom', 'hid'), may hold values from -6 to 6
- grad_out: bfloat16 [393216, 512], P('dom', 'hid'), may hold values from -6 to 6
- w_self: bfloat16 [512, 512], P('hid'), may hold values from -0.25 to 0.25
- w_neigh: bfloat16 [512, 512], P('hid'), may hold values from -0.25 to 0.25
- adj_tiles: bfloat16 [6144, 128, 128], P('dom'), may hold values from 0 to 8, as said below
- tile_row: int32 [6144], P('dom'), may hold values from 0 to 95
- tile_col: int32 [6144], P('dom'), may hold values from 0 to 95
- tile_owner: int32 [6144, 1], P('dom'), may hold values from 0 to 31; in each aligned block of 192 rows (0 to 191, 192 to 383, ...) at most 12 rows name the same one
- in_degree: int32 [393216], P('dom'), may hold values from 16 to 128
Outputs:
- grad_feats: bfloat16 [393216, 512], P('dom', 'hid')
- grad_w_self: float32 [512, 512], P('hid')
- grad_w_neigh: float32 [512, 512], P('hid')
- grad_bias: float32 [512], P('hid')
Inputs may be any that keep to these rules, and one draw needn't show every extreme that they name: `tile_owner`: among the tiles of one partition no owner is named more than 12 times, a bound that some block reaches. `adj_tiles`: each entry is 0 or lies between 0.5 and 8.
All inputs are finite; a program needn't handle non-finite values.
Results may differ from a plain program's by a relative error of at most 0.0053.
Values may be sent and summed in bfloat16 or wider, within the bound.
No kernel may reach another device: no remote copies, remote signals or barrier semaphores. Data moves between devices by JAX's collectives and lax.ppermute only.
A program may use at most 192 MiB of HBM per device.

v0:
```python
import math

import jax
import jax.numpy as jnp
from jax import lax
from jax.sharding import PartitionSpec as P


def local(
    features,
    neigh_mean,
    pre_relu,
    grad_out,
    w_self,
    w_neigh,
    adj_tiles,
    tile_row,
    tile_col,
    tile_owner,
    in_degree,
):
    dom_count = lax.axis_size("dom")
    rows_here = features.shape[0]
    width_part = features.shape[1]
    tile_size = adj_tiles.shape[1]
    block_count = rows_here // tile_size
    tile_count = adj_tiles.shape[0]
    capacity = max(2, 2 * tile_count // dom_count)
    slot_total = dom_count * capacity
    grad_scale = 1.0 / math.sqrt(rows_here * dom_count)
    contract = (((1,), (1,)), ((), ()))
    over_rows = (((0,), (0,)), ((), ()))
    local_grad = jnp.where(pre_relu > 0, grad_out, jnp.zeros_like(grad_out))
    full_grad = lax.all_gather(local_grad, "hid", axis=1, tiled=True)
    self_term = lax.dot_general(full_grad, w_self, contract, preferred_element_type=jnp.float32)
    part_self = lax.dot_general(features, full_grad, over_rows, preferred_element_type=jnp.float32)
    part_neigh = lax.dot_general(
        neigh_mean, full_grad, over_rows, preferred_element_type=jnp.float32
    )
    part_bias = jnp.sum(local_grad.astype(jnp.float32), axis=0)
    totals = lax.psum((part_self, part_neigh, part_bias), "dom")
    self_term, totals = (self_term, totals)
    pushed = lax.dot_general(full_grad, w_neigh, contract, preferred_element_type=jnp.float32)
    scaled = (pushed / in_degree.astype(jnp.float32)[:, None]).astype(jnp.bfloat16)
    chosen = scaled.reshape(block_count, tile_size, width_part)[tile_row]
    owners = tile_owner[:, 0]
    owner_marks = (owners[:, None] == jnp.arange(dom_count, dtype=jnp.int32)[None, :]).astype(
        jnp.int32
    )
    earlier = jnp.cumsum(owner_marks, axis=0) - owner_marks
    slot_rank = jnp.sum(earlier * owner_marks, axis=1)
    slot_index = owners * capacity + slot_rank
    slot_cols = jnp.full((slot_total,), -1, jnp.int32).at[slot_index].set(tile_col)
    messages = jnp.einsum(
        "tij,tif->tjf", adj_tiles, chosen, preferred_element_type=jnp.float32
    ).astype(jnp.bfloat16)
    outgoing = (
        jnp.zeros((slot_total, tile_size, width_part), jnp.bfloat16).at[slot_index].set(messages)
    )
    received = lax.all_to_all(
        outgoing.reshape(dom_count, capacity, tile_size, width_part),
        "dom",
        split_axis=0,
        concat_axis=0,
        tiled=True,
    )
    in_cols = lax.all_to_all(
        slot_cols.reshape(dom_count, capacity), "dom", split_axis=0, concat_axis=0, tiled=True
    )
    received = received.reshape(slot_total, tile_size * width_part)
    col_picks = (
        in_cols.reshape(1, slot_total) == jnp.arange(block_count, dtype=jnp.int32)[:, None]
    ).astype(jnp.bfloat16)
    summed = jnp.dot(col_picks, received, preferred_element_type=jnp.float32)
    neighbour = summed.reshape(rows_here, width_part)
    grad_feats = (self_term + neighbour).astype(jnp.bfloat16)
    return (grad_feats, totals[0] * grad_scale, totals[1] * grad_scale, totals[2] * grad_scale)


def solution(mesh):
    return jax.shard_map(
        local,
        mesh=mesh,
        in_specs=(
            P("dom", "hid"),
            P("dom", "hid"),
            P("dom", "hid"),
            P("dom", "hid"),
            P("hid", None),
            P("hid", None),
            P("dom", None, None),
            P("dom"),
            P("dom"),
            P("dom", None),
            P("dom"),
        ),
        out_specs=(P("dom", "hid"), P("hid", None), P("hid", None), P("hid")),
        check_vma=False,
    )
```

profile of v0, /device:TPU:1, one launch (start us, length us, event | category | flops | bytes accessed | tf_op | source)
XLA Modules:
  0.0 477.2 jit_solution(14503556164753101941)
XLA Ops:
  7.2 0.0 copy-start
  7.2 0.0 copy-start.3
  7.2 0.0 copy-start.2
  7.2 0.0 copy-start.4
  7.2 0.0 copy-start.6
  7.2 0.0 all-gather.2.cloned.1.call-start
  7.3 4.9 %convert_reduce_fusion = (f32[128]{0:T(128)S(1)}, bf16[12288,128]{1,0:T(8,128)(2,1)}) fusion(bf16[12288,128]{1,0:T(8,128)(2,1)} %param.14, bf16[12288,128]{1,0:T(8,128)(2,1)} %param.13), kind=kLoop, calls=%fused_computation.10 | loop fusion | flops 6291328 | bytes 9437696 | tf_op jit(solution)/shard_map/reduce_sum | solution.py:40
  12.1 0.0 all-gather.2.cloned.1.call-update
  12.2 0.0 copy-done.3
  12.2 0.6 reduce-window.6
  12.8 0.2 slice_reduce_fusion
  13.0 0.1 bitcast_bitcast_fusion
  13.2 1.4 scatter_custom_fusion
  14.5 0.7 all_to_all.9
  15.2 9.4 %all-to-all-start = ((s32[32,1,12]{2,1,0:T(1,128)}), s32[32,1,12]{2,1,0:T(1,128)S(1)}, u32[]{:S(2)}, u32[]{:S(2)}) async-start(s32[32,1,12]{2,1,0:T(1,128)} %bitcast.4), calls=%async_computation | async-start | bytes 32768 | tf_op jit(solution)/shard_map/all_to_all | solution.py:67
  24.7 0.0 copy-done.2
  24.7 0.0 copy-done.4
  24.7 112.8 %all-gather.2.cloned.1.call-done = bf16[12288,512]{1,0:T(8,128)(2,1)} async-done(((bf16[12288,128]{1,0:T(8,128)(2,1)}), bf16[12288,512]{1,0:T(8,128)(2,1)}) %all-gather.2.cloned.1.call-update) | async-done | bytes 12582928 | tf_op jit(solution)/shard_map/all_gather | solution.py:34
  137.6 0.0 copy-done.6
  137.6 7.6 %fusion.1 = bf16[12288,128]{1,0:T(8,128)(2,1)} fusion(bf16[12288,512]{1,0:T(8,128)(2,1)} %all-gather.2.cloned.1.call-done, bf16[128,512]{1,0:T(8,128)(2,1)S(1)} %copy-done.6, f32[12288]{0:T(1024)S(1)} %convert_element_type.24), kind=kOutput, calls=%fused_computation.6 | convolution fusion | flops 1613758464 | bytes 15908864 | tf_op jit(solution)/shard_map/dot_general | solution.py:43
  145.1 9.9 %gather_fusion = bf16[192,128,128]{2,1,0:T(8,128)(2,1)} fusion(bf16[96,128,128]{2,1,0:T(8,128)(2,1)} %bitcast.40, s32[1024]{0:T(1024)S(1)} %pad_clamp_fusion), kind=kCustom, calls=%fused_computation | custom fusion | bytes 12583680 | tf_op jit(solution)/shard_map/gather | solution.py:45
  155.0 9.4 %convert_bitcast_fusion = bf16[192,128,128]{1,2,0:T(8,128)(2,1)} fusion(bf16[192,128,128]{2,1,0:T(8,128)(2,1)} %gather_fusion, bf16[192,128,128]{2,1,0:T(8,128)(2,1)} %param.17), kind=kOutput, calls=%fused_computation.11 | convolution fusion | flops 808452096 | bytes 18874368 | tf_op jit(solution)/shard_map/tij,tif->tjf/dot_general | solution.py:54
  164.4 8.7 %copy.28 = bf16[192,128,128]{2,1,0:T(8,128)(2,1)} copy(bf16[192,128,128]{1,2,0:T(8,128)(2,1)} %convert_bitcast_fusion) | data formatting | bytes 12582912 | tf_op jit(solution)/shard_map/convert_element_type | solution.py:56
  173.1 7.8 %broadcast_in_dim.7 = bf16[384,128,128]{2,1,0:T(8,128)(2,1)} broadcast(bf16[]{:T(256)} %constant.9.clone.1), dimensions={} | broadcast | bytes 12582914 | tf_op jit(solution)/shard_map/broadcast_in_dim | solution.py:58
  180.9 28.7 %scatter_fusion = bf16[384,128,128]{2,1,0:T(8,128)(2,1)} fusion(bf16[384,128,128]{2,1,0:T(8,128)(2,1)} %broadcast_in_dim.7, s32[192]{0:T(256)S(1)} %bitcast.44, bf16[192,128,128]{2,1,0:T(8,128)(2,1)} %copy.28), kind=kCustom, calls=%fused_computation.2 | custom fusion | bytes 18875136 | tf_op jit(solution)/shard_map/scatter | solution.py:58
  209.6 0.0 all-to-all-done
  209.6 8.6 %all-to-all-start.1 = ((bf16[32,12,128,128]{3,2,1,0:T(8,128)(2,1)}), bf16[32,12,128,128]{3,2,1,0:T(8,128)(2,1)}, u32[]{:S(2)}, u32[]{:S(2)}) async-start(bf16[32,12,128,128]{3,2,1,0:T(8,128)(2,1)} %bitcast.39), calls=%async_computation.1 | async-start | bytes 25165824 | tf_op jit(solution)/shard_map/all_to_all | solution.py:60
  218.2 0.0 all-reduce.4.cloned.1.call-start
  218.3 0.0 copy-done
  218.3 0.0 copy-start.5
  218.3 7.3 %convolution_bitcast_fusion = f32[128,512]{0,1:T(8,128)} fusion(bf16[12288,512]{1,0:T(8,128)(2,1)} %all-gather.2.cloned.1.call-done, bf16[12288,128]{1,0:T(8,128)(2,1)S(1)} %copy-done), kind=kOutput, calls=%fused_computation.13 | convolution fusion | flops 1610612736 | bytes 15990784 | tf_op jit(solution)/shard_map/dot_general | solution.py:37
  225.6 0.0 copy-done.5
  225.6 7.2 %convolution_bitcast_fusion.1 = f32[128,512]{0,1:T(8,128)} fusion(bf16[12288,512]{1,0:T(8,128)(2,1)} %all-gather.2.cloned.1.call-done, bf16[12288,128]{1,0:T(8,128)(2,1)S(1)} %copy-done.5), kind=kOutput, calls=%fused_computation.14 | convolution fusion | flops 1610612736 | bytes 15990784 | tf_op jit(solution)/shard_map/dot_general | solution.py:36
  232.8 0.0 all-reduce.4.cloned.1.call-update
  232.9 195.9 %psum.23 = f32[128]{0:T(128)S(1)} all-reduce(f32[128]{0:T(128)S(1)} %get-tuple-element.18), channel_id=1, replica_groups=mesh['dom'=32,'hid'=4] {'dom'}, use_global_device_ids=true, to_apply=%region_8.9 | all-reduce | flops 128 | bytes 1024 | tf_op jit(solution)/shard_map/psum | solution.py:41
  428.8 0.5 broadcast_multiply_fusion.2
  429.3 0.5 broadcast.52
  429.8 0.7 reduce.5
  430.5 0.1 eq.44
  430.6 1.8 all-reduce.4.cloned.1.call-done
  432.4 1.8 broadcast_multiply_fusion
  434.2 1.8 copy.29
  436.0 0.8 copy.30
  436.8 0.0 all-to-all-done.1
  436.8 14.9 %fusion.2 = f32[96,16384]{1,0:T(8,128)} fusion(bf16[48,8,128,128]{3,2,1,0:T(8,128)(2,1)} %bitcast.15, s32[384]{0:T(512)S(1)} %eq.44), kind=kOutput, calls=%fused_computation.7 | convolution fusion | flops 1207996416 | bytes 18875904 | tf_op jit(solution)/shard_map/dot_general | solution.py:74
  451.8 0.0 copy-start.1
  451.8 7.1 %reshape.45 = f32[12288,128]{1,0:T(8,128)} reshape(f32[96,16384]{1,0:T(8,128)} %fusion.2) | data formatting | bytes 12582912 | tf_op jit(solution)/shard_map/reshape | solution.py:75
  458.9 0.0 copy-done.1
  458.9 11.5 %fusion = bf16[12288,128]{1,0:T(8,128)(2,1)} fusion(f32[12288,128]{1,0:T(8,128)} %reshape.45, bf16[12288,512]{1,0:T(8,128)(2,1)} %all-gather.2.cloned.1.call-done, bf16[128,512]{1,0:T(8,128)(2,1)S(1)} %copy-done.1), kind=kOutput, calls=%fused_computation.4 | convolution fusion | flops 1613758464 | bytes 22151168 | tf_op jit(solution)/shard_map/dot_general | solution.py:35
  (9 shorter events, 0.1 us)
Async XLA Ops:
  7.2 211.1 %copy-start = (bf16[12288,128]{1,0:T(8,128)(2,1)S(1)}, bf16[12288,128]{1,0:T(8,128)(2,1)}, u32[]{:S(2)}) copy-start(bf16[12288,128]{1,0:T(8,128)(2,1)} %param.12) | copy-start | bytes 9437188
  7.2 5.0 %copy-start.3 = (s32[192,1]{0,1:T(1,128)S(1)}, s32[192,1]{0,1:T(1,128)}, u32[]{:S(2)}) copy-start(s32[192,1]{0,1:T(1,128)} %param.20) | copy-start | bytes 2308
  7.2 17.5 %copy-start.2 = (s32[12288]{0:T(1024)S(1)}, s32[12288]{0:T(1024)}, u32[]{:S(2)}) copy-start(s32[12288]{0:T(1024)} %param.21) | copy-start | bytes 147460
  7.2 17.5 %copy-start.4 = (s32[192]{0:T(256)S(1)}, s32[192]{0:T(256)}, u32[]{:S(2)}) copy-start(s32[192]{0:T(256)} %param.18) | copy-start | bytes 2308
  7.2 130.4 %copy-start.6 = (bf16[128,512]{1,0:T(8,128)(2,1)S(1)}, bf16[128,512]{1,0:T(8,128)(2,1)}, u32[]{:S(2)}) copy-start(bf16[128,512]{1,0:T(8,128)(2,1)} %param.16) | copy-start | bytes 393220
  7.2 130.3 %all-gather.2.cloned.1.call-start = ((), (), s32[]{:S(2)}) async-start(), calls=%async_computation.2 | async-start | bytes 15728640 | tf_op jit(solution)/shard_map/all_gather | solution.py:34
  15.2 194.4 %all-to-all-start = ((s32[32,1,12]{2,1,0:T(1,128)}), s32[32,1,12]{2,1,0:T(1,128)S(1)}, u32[]{:S(2)}, u32[]{:S(2)}) async-start(s32[32,1,12]{2,1,0:T(1,128)} %bitcast.4), calls=%async_computation | async-start | bytes 32768 | tf_op jit(solution)/shard_map/all_to_all | solution.py:67
  209.6 227.2 %all-to-all-start.1 = ((bf16[32,12,128,128]{3,2,1,0:T(8,128)(2,1)}), bf16[32,12,128,128]{3,2,1,0:T(8,128)(2,1)}, u32[]{:S(2)}, u32[]{:S(2)}) async-start(bf16[32,12,128,128]{3,2,1,0:T(8,128)(2,1)} %bitcast.39), calls=%async_computation.1 | async-start | bytes 25165824 | tf_op jit(solution)/shard_map/all_to_all | solution.py:60
  218.2 214.2 %all-reduce.4.cloned.1.call-start = ((), (), s32[]{:S(2)}) async-start(), calls=%async_computation.3 | async-start | bytes 1048576 | tf_op jit(solution)/shard_map/psum | solution.py:41
  218.3 7.3 %copy-start.5 = (bf16[12288,128]{1,0:T(8,128)(2,1)S(1)}, bf16[12288,128]{1,0:T(8,128)(2,1)}, u32[]{:S(2)}) copy-start(bf16[12288,128]{1,0:T(8,128)(2,1)} %param.11) | copy-start | bytes 9437188
  451.8 7.1 %copy-start.1 = (bf16[128,512]{1,0:T(8,128)(2,1)S(1)}, bf16[128,512]{1,0:T(8,128)(2,1)}, u32[]{:S(2)}) copy-start(bf16[128,512]{1,0:T(8,128)(2,1)} %param.15) | copy-start | bytes 393220
Sparse Core Ops, SparseCore 0:
  12.3 125.2 all-gather.1
  233.0 199.4 all-reduce.3
where the time goes:
time: 478 us; the launch traced here: 477 us
  blocking collectives  196 us (41%)
  waiting for transfers between devices  115 us (24%)
  local copies, waits for them, and re-layouts  67.8 us (14%)
  matrix products  57.9 us (12%)
  starting transfers between devices  18.1 us (4%)
  between operations  14.2 us (3%)
  other arithmetic  8.63 us (2%)
    psum x1, blocking collectives, local(): totals = lax.psum((part_self, part_neigh, part_bias), 'dom')  196 us
    all_gather x1, waiting for transfers between devices, local(): full_grad = lax.all_gather(local_grad, 'hid', axis=1, tiled=True)  113 us
    scatter x1, local copies, waits for them, and re-layouts, local(): jnp.zeros((slot_total, tile_size, width_part), jnp.bfloat16).at[slot_index]  28.7 us
    dot_general x1, matrix products, local(): summed = jnp.dot(col_picks, received, preferred_element_type=jnp.float32)  14.9 us
    dot_general x1, matrix products, local(): lax.dot_general(full_grad, w_self, contract, preferred_element_type=jnp.f...  11.5 us
    gather x1, local copies, waits for them, and re-layouts, local(): chosen = scaled.reshape(block_count, tile_size, width_part)[tile_row]  9.89 us
  transfers between devices with their start and end apart: 4, of which 2 were waited for; matrix products, arithmetic and copies ran while one was open for 20% of the time, Pallas kernels for 0%

commit v1 on v0

v1 whole, which is shorter than its diff:
```python
import functools
import math

import jax
import jax.numpy as jnp
from jax import lax
from jax.experimental import pallas as pl
from jax.experimental.pallas import tpu as pltpu
from jax.sharding import PartitionSpec as P

BLK = 128
CAP = 12
HEAD = 96
TAIL = BLK - HEAD
MARK = 16
CHUNK = 2048
WROWS = 48
GROUP = 8
SLICES = 3
VMEM = 40 * 1024 * 1024
F32, BF16 = jnp.float32, jnp.bfloat16


def params():
    return pltpu.CompilerParams(
        dimension_semantics=("arbitrary",), vmem_limit_bytes=VMEM
    )


def cost(flops, size):
    return pl.CostEstimate(flops=flops // 1000, bytes_accessed=size // 1000, transcendentals=0)


def lanes(start, size):
    return pl.ds(pl.multiple_of(start, BLK), size)


def message_kernel(tile_ids, row_ids, grad, degree, far, cols, head, tail, rows, tiles, sem):
    step = pl.program_id(0)

    @pl.when(step == 0)
    def _():
        fetch = pltpu.make_async_copy(far, tiles, sem)
        fetch.start()

        def turn(b, carry):
            at = lanes(b * BLK, BLK)
            turned = grad[at, :].T.astype(F32)
            rows[:, at] = (turned * (1.0 / degree[:, at].astype(F32))).astype(BF16)
            return carry

        lax.fori_loop(0, grad.shape[0] // BLK, turn, 0, unroll=8)
        fetch.wait()

    def one(g, carry):
        base = (step * GROUP + g) * CAP
        for k in range(CAP):
            picked = rows[:, lanes(row_ids[base + k] * BLK, BLK)]
            message = jnp.dot(picked, tiles[tile_ids[base + k]], preferred_element_type=F32)
            message = message.astype(BF16)
            head[g, k * HEAD : (k + 1) * HEAD, :] = message[:HEAD]
            tail[g, k * TAIL : (k + 1) * TAIL, :] = message[HEAD:]
        return carry

    lax.fori_loop(0, GROUP, one, 0)
    head[:, CAP * HEAD :, :] = cols[...]


def messages(tile_ids, row_ids, grad, degree, tiles, cols):
    owners, hosts = cols.shape[0], grad.shape[0]
    whole = pl.BlockSpec(memory_space=pltpu.VMEM)

    def group(height):
        return pl.BlockSpec((GROUP, height, BLK), lambda o, *_: (o, 0, 0))

    heights = (CAP * HEAD + MARK, CAP * TAIL)
    return pl.pallas_call(
        message_kernel,
        grid_spec=pltpu.PrefetchScalarGridSpec(
            num_scalar_prefetch=2,
            grid=(owners // GROUP,),
            in_specs=[whole, whole, pl.BlockSpec(memory_space=pl.ANY), group(MARK)],
            out_specs=[group(h) for h in heights],
            scratch_shapes=[
                pltpu.VMEM((BLK, hosts), BF16),
                pltpu.VMEM(tiles.shape, BF16),
                pltpu.SemaphoreType.DMA,
            ],
        ),
        out_shape=[jax.ShapeDtypeStruct((owners, h, BLK), BF16) for h in heights],
        compiler_params=params(),
        cost_estimate=cost(2 * owners * CAP * BLK**3, 21 << 20),
        name="messages",
    )(tile_ids, row_ids, grad, degree, tiles, cols)


def sum_kernel(height, parts, col_ids, place, received, *rest):
    weights, outs, total = rest[: -parts - 1], rest[-parts - 1 : -1], rest[-1]
    step = pl.program_id(0)

    @pl.when(step == 0)
    def _():
        total[...] = jnp.zeros_like(total)

    def one(g, carry):
        base = (step * GROUP + g) * CAP
        for k in range(CAP):
            at = lanes(col_ids[base + k] * BLK, BLK)
            total[:, at] += received[g, k * height : (k + 1) * height, :].astype(F32)
        return carry

    lax.fori_loop(0, GROUP, one, 0)

    @pl.when(step == pl.num_programs(0) - 1)
    def _():
        width = outs[0].shape[1]
        for k, out in enumerate(outs):
            to = lax.rem(place[0] + k, parts)
            out[:height, :] = total[:, lanes(to * width, width)].astype(BF16)
            for weight in weights:
                units = weight.shape[1]
                for i, r in enumerate(range(0, weight.shape[0], WROWS)):
                    piece = weight[r : r + WROWS, :]
                    out[height : height + piece.shape[0], i * units : (i + 1) * units] = piece


def unit_sums(height, col_ids, place, received, blocks, parts, weight=None):
    sources = received.shape[0]
    width = blocks * BLK // parts
    extra = [] if weight is None else [weight]
    shape = (height + WROWS * len(extra), width)
    return pl.pallas_call(
        functools.partial(sum_kernel, height, parts),
        grid_spec=pltpu.PrefetchScalarGridSpec(
            num_scalar_prefetch=2,
            grid=(sources // GROUP,),
            in_specs=[pl.BlockSpec((GROUP, CAP * height, BLK), lambda p, *_: (p, 0, 0))]
            + [pl.BlockSpec(memory_space=pltpu.VMEM)] * len(extra),
            out_specs=[pl.BlockSpec(shape, lambda p, *_: (0, 0))] * parts,
            scratch_shapes=[pltpu.VMEM((height, (blocks + 1) * BLK), F32)],
        ),
        out_shape=[jax.ShapeDtypeStruct(shape, BF16)] * parts,
        compiler_params=params(),
        cost_estimate=cost(sources * CAP * height * BLK, 9 << 20),
        name="unit_sums",
    )(col_ids, place, received, *extra)


def turn_kernel(place, *rest):
    parts = (len(rest) - 3) // 3
    heads, tails, grad = rest[:parts], rest[parts : 2 * parts], rest[2 * parts]
    outs, near, own = rest[2 * parts + 1 : -2], rest[-2], rest[-1]
    units = grad.shape[1]
    chunk = outs[0].shape[0]
    step = pl.program_id(0)

    @pl.when(step == 0)
    def _():
        for k in range(parts):
            sender = heads[(parts - k) % parts]
            rows = [
                sender[HEAD : HEAD + min(WROWS, 2 * BLK - r), i * units : (i + 1) * units]
                for i, r in enumerate(range(0, 2 * BLK, WROWS))
            ]
            both = jnp.concatenate(rows, axis=0)
            own[:, k * BLK : (k + 1) * BLK] = both[BLK:].T
            near[k * BLK : (k + 1) * BLK, :] = both[:BLK]

        for k in range(parts):
            rows = slice(k * BLK, (k + 1) * BLK)
            blocks = [
                near[rows, lanes(lax.rem(place[0] + parts - i, parts) * BLK, BLK)]
                for i in range(parts)
            ]
            near[rows, :] = jnp.concatenate(blocks, axis=1)

    at = lanes(step * chunk, chunk)
    sums = []
    for head, tail in zip(heads, tails):
        sums += [head[:HEAD, at], tail[:, at]]
    turned = jnp.dot(near[...], jnp.concatenate(sums, axis=0), preferred_element_type=F32)
    result = jnp.dot(grad[...], own[...], preferred_element_type=F32)
    for k, out in enumerate(outs):
        part = result[:, k * BLK : (k + 1) * BLK] + turned[k * BLK : (k + 1) * BLK, :].T
        out[...] = part.astype(BF16)


def turn(place, heads, tails, grad):
    parts, width = len(heads), tails[0].shape[1]
    units = grad.shape[1]
    chunk = width // SLICES
    whole = pl.BlockSpec(memory_space=pltpu.VMEM)
    return pl.pallas_call(
        turn_kernel,
        grid_spec=pltpu.PrefetchScalarGridSpec(
            num_scalar_prefetch=1,
            grid=(SLICES,),
            in_specs=[whole] * (2 * parts)
            + [pl.BlockSpec((chunk, units), lambda i, place: (place[0] * SLICES + i, 0))],
            out_specs=[pl.BlockSpec((chunk, BLK), lambda i, *_: (i, 0))] * parts,
            scratch_shapes=[pltpu.VMEM((units, units), BF16)] * 2,
        ),
        out_shape=[jax.ShapeDtypeStruct((width, BLK), BF16)] * parts,
        compiler_params=params(),
        cost_estimate=cost(4 * units * units * width, 10 << 20),
        name="turn",
    )(place, *heads, *tails, grad)


def weight_kernel(place, first, second, grad, out, total, bias):
    step = pl.program_id(0)
    both = jnp.concatenate([first[...], second[...]], axis=1)
    part = lax.dot_general(both, grad[...], (((0,), (0,)), ((), ())), preferred_element_type=F32)
    ones = jnp.ones((8, grad.shape[0]), BF16)
    column = jnp.dot(ones, grad[...], preferred_element_type=F32)

    @pl.when(step == 0)
    def _():
        total[...] = part
        bias[...] = column

    @pl.when(step > 0)
    def _():
        total[...] += part
        bias[...] += column

    @pl.when(step == pl.num_programs(0) - 1)
    def _():
        mine = bias[:, lanes(place[0] * BLK, BLK)]
        quarters = total.shape[1] // BLK
        for o in range(out.shape[0]):
            for q in range(quarters):
                out[o, 8 * q : 8 * q + 8, :] = total[8 * o : 8 * o + 8, BLK * q : BLK * q + BLK]
            out[o, 8 * quarters :, :] = mine


def weight_parts(place, first, second, grad, owners):
    hosts, units = grad.shape
    height = 8 * (units // BLK) + 8
    piece = pl.BlockSpec((CHUNK, BLK), lambda i, *_: (i, 0))
    return pl.pallas_call(
        weight_kernel,
        grid_spec=pltpu.PrefetchScalarGridSpec(
            num_scalar_prefetch=1,
            grid=(hosts // CHUNK,),
            in_specs=[piece, piece, pl.BlockSpec((CHUNK, units), lambda i, *_: (i, 0))],
            out_specs=pl.BlockSpec((owners, height, BLK), lambda i, *_: (0, 0, 0)),
            scratch_shapes=[pltpu.VMEM((2 * BLK, units), F32), pltpu.VMEM((8, units), F32)],
        ),
        out_shape=jax.ShapeDtypeStruct((owners, height, BLK), F32),
        compiler_params=params(),
        cost_estimate=cost(4 * BLK * hosts * units, 19 << 20),
        name="weight_parts",
    )(place, first, second, grad)


def place_kernel(place, *rest):
    pieces, out = rest[:-1], rest[-1]
    for k, piece in enumerate(pieces):

        @pl.when(pl.program_id(0) == k)
        def _():
            out[...] = piece[...]


def place_quarters(place, pieces):
    parts, (width, features) = len(pieces), pieces[0].shape
    return pl.pallas_call(
        place_kernel,
        grid_spec=pltpu.PrefetchScalarGridSpec(
            num_scalar_prefetch=1,
            grid=(parts,),
            in_specs=[pl.BlockSpec(memory_space=pltpu.VMEM)] * parts,
            out_specs=pl.BlockSpec(
                (width, features), lambda k, place: (lax.rem(place[0] + parts - k, parts), 0)
            ),
        ),
        out_shape=jax.ShapeDtypeStruct((parts * width, features), BF16),
        compiler_params=params(),
        cost_estimate=cost(0, 6 << 20),
        name="place_quarters",
    )(place, *pieces)


def exchange(pieces):
    parts = len(pieces)
    moved = [pieces[0]]
    for k in range(1, parts):
        moved.append(lax.ppermute(pieces[k], "hid", [(i, (i + k) % parts) for i in range(parts)]))
    return moved


def swap(array):
    return lax.all_to_all(array, "dom", split_axis=0, concat_axis=0, tiled=True)


def local(
    features,
    neigh_mean,
    pre_relu,
    grad_out,
    w_self,
    w_neigh,
    adj_tiles,
    tile_row,
    tile_col,
    tile_owner,
    in_degree,
):
    owners = lax.axis_size("dom")
    parts = lax.axis_size("hid")
    hosts = features.shape[0]
    blocks = hosts // BLK
    tile_count = adj_tiles.shape[0]
    slots = owners * CAP
    scale = 1.0 / math.sqrt(hosts * owners)
    place = lax.axis_index("hid").astype(jnp.int32).reshape(1)
    degree = in_degree.reshape(1, hosts)

    grad = jnp.where(pre_relu > 0, grad_out, jnp.zeros_like(grad_out))
    full_grad = lax.all_gather(grad, "hid", axis=1, tiled=True)

    owner = tile_owner[:, 0]
    order = jnp.arange(tile_count, dtype=jnp.int32)
    before = (owner[:, None] == owner[None, :]) & (order[None, :] < order[:, None])
    slot = owner * CAP + jnp.sum(before.astype(jnp.int32), axis=1)
    hit = jnp.arange(slots, dtype=jnp.int32)[:, None] == slot[None, :]
    tile_ids = jnp.sum(jnp.where(hit, order[None, :], 0), axis=1)
    row_ids = jnp.sum(jnp.where(hit, tile_row[None, :], 0), axis=1)
    col_ids = blocks + jnp.sum(jnp.where(hit, tile_col[None, :] - blocks, 0), axis=1)
    cols = jnp.pad(
        col_ids.astype(BF16).reshape(owners, 1, CAP), ((0, 0), (0, MARK - 1), (0, BLK - CAP))
    )

    head, tail = messages(tile_ids, row_ids, grad, degree, adj_tiles, cols)
    weights = jnp.concatenate([w_neigh, w_self], axis=0)
    head, tail, place, weights = lax.optimization_barrier((head, tail, place, weights))
    head = swap(head)
    col_ids = head[:, CAP * HEAD, :CAP].astype(jnp.int32).reshape(slots)
    heads = unit_sums(HEAD, col_ids, place, head, blocks, parts, weights)
    heads, tail, full_grad = lax.optimization_barrier((heads, tail, full_grad))
    heads = exchange(heads)
    tails = unit_sums(TAIL, col_ids, place, swap(tail), blocks, parts)
    tails = exchange(tails)

    pieces = weight_parts(place, features, neigh_mean, full_grad, owners)
    quarters = turn(place, heads, tails, full_grad)
    pieces, quarters = lax.optimization_barrier((pieces, quarters))
    quarters = exchange(quarters)
    summed = jnp.sum(swap(pieces), axis=0)
    rows = 8 * parts
    gathered = swap(jnp.broadcast_to(summed[:rows], (owners, rows, BLK)))
    grads = gathered.reshape(owners, parts, 8, BLK).transpose(0, 2, 1, 3)
    grads = grads.reshape(2 * BLK, parts * BLK) * scale
    bias = summed[rows] * scale

    return place_quarters(place, quarters), grads[:BLK], grads[BLK:], bias


def solution(mesh):
    return jax.shard_map(
        local,
        mesh=mesh,
        in_specs=(
            P("dom", "hid"),
            P("dom", "hid"),
            P("dom", "hid"),
            P("dom", "hid"),
            P("hid", None),
            P("hid", None),
            P("dom", None, None),
            P("dom"),
            P("dom"),
            P("dom", None),
            P("dom"),
        ),
        out_specs=(P("dom", "hid"), P("hid", None), P("hid", None), P("hid")),
        check_vma=False,
    )
```

time: 478 us -> 292 us (0.61)
  blocking collectives: 196 us -> 118 us
  matrix products: 57.9 us -> 0 us
  waiting for transfers between devices: 115 us -> 61.4 us
  local copies, waits for them, and re-layouts: 67.8 us -> 19.9 us
  Pallas kernels: 0 us -> 40.4 us
  starting transfers between devices: 18.1 us -> 30.1 us
    psum x1 -> x0, blocking collectives: 196 us -> none  [local(): totals = lax.psum((part_self, part_neigh, part_bias), 'dom')]
    all_to_all x0 -> x1, blocking collectives: none -> 118 us  [swap(): return lax.all_to_all(array, 'dom', split_axis=0, concat_axis=0, tiled=True)]
    all_gather x1, waiting for transfers between devices: 113 us -> 0.01 us  [local(): full_grad = lax.all_gather(grad, 'hid', axis=1, tiled=True)]
    dot_general x6 -> x0, matrix products: 57.9 us -> none  [the longest x1 14.9 us: local(): summed = jnp.dot(col_picks, received, preferred_element_type=jnp.float32)]
    all_to_all x2 -> x3, waiting for transfers between devices: 0.01 us -> 44.3 us  [swap(): return lax.all_to_all(array, 'dom', split_axis=0, concat_axis=0, tiled=True)]
    pallas_call x0 -> x6, Pallas kernels: none -> 40.4 us  [the longest x1 12.7 us: messages(): pl.pallas_call(message_kernel, grid_spec=pltpu.PrefetchScalarGridSpec(num...]
    scatter x2 -> x0, local copies, waits for them, and re-layouts: 30.1 us -> none  [the longest x1 28.7 us: local(): jnp.zeros((slot_total, tile_size, width_part), jnp.bfloat16).at[slot_index]]
    ppermute x0 -> x9, waiting for transfers between devices: none -> 17.1 us  [exchange(): lax.ppermute(pieces[k], 'hid', [(i, (i + k) % parts) for i in range(parts)])]
  transfers between devices with their start and end apart: 4 -> 13, of which waited for: 2 -> 4; matrix products, arithmetic and copies ran while one was open for 20% -> 1% of each run, Pallas kernels for 0% -> 11%
where the time goes in v1:
time: 292 us
  blocking collectives  118 us (40%)
  waiting for transfers between devices  61.4 us (21%)
  Pallas kernels  40.4 us (14%)
  starting transfers between devices  30.1 us (10%)
  local copies, waits for them, and re-layouts  19.9 us (7%)
  between operations  14.3 us (5%)
  other arithmetic  7.34 us (3%)
    all_to_all x1, blocking collectives, swap(): return lax.all_to_all(array, 'dom', split_axis=0, concat_axis=0, tiled=True)  118 us
    all_to_all x3, waiting for transfers between devices, swap(): return lax.all_to_all(array, 'dom', split_axis=0, concat_axis=0, tiled=True)  44.3 us
    unnamed x38, local copies, waits for them, and re-layouts  18 us
    all_to_all x3, starting transfers between devices, swap(): return lax.all_to_all(array, 'dom', split_axis=0, concat_axis=0, tiled=True)  17.1 us
    ppermute x9, waiting for transfers between devices, exchange(): lax.ppermute(pieces[k], 'hid', [(i, (i + k) % parts) for i in range(parts)])  17.1 us
    ppermute x9, starting transfers between devices, exchange(): lax.ppermute(pieces[k], 'hid', [(i, (i + k) % parts) for i in range(parts)])  13 us
    pallas_call x1, Pallas kernels, messages(): pl.pallas_call(message_kernel, grid_spec=pltpu.PrefetchScalarGridSpec(num...  12.7 us
    pallas_call x1, Pallas kernels, weight_parts(): pl.pallas_call(weight_kernel, grid_spec=pltpu.PrefetchScalarGridSpec(num_...  10.1 us
  transfers between devices with their start and end apart: 13, of which 4 were waited for; matrix products, arithmetic and copies ran while one was open for 1% of the time, Pallas kernels for 11%

profile of v1, /device:TPU:1, one launch (start us, length us, event | category | flops | bytes accessed | tf_op | source)
XLA Modules:
  0.0 291.7 jit_solution(4043754670487483282)
XLA Ops:
  7.2 0.0 all-gather.2.cloned.1.call-start
  7.2 0.0 copy-start.16
  7.2 0.0 copy-start.17
  7.2 0.0 copy-start.18
  7.2 4.2 %compare_select_fusion.grad = bf16[12288,128]{1,0:T(8,128)(2,1)} fusion(bf16[12288,128]{1,0:T(8,128)(2,1)} %param.14, bf16[12288,128]{1,0:T(8,128)(2,1)} %param.13), kind=kLoop, calls=%fused_computation | loop fusion | flops 3145728 | bytes 9437184 | tf_op jit(solution)/shard_map/jit(_where)/select_n | solution.py:320
  11.4 0.0 all-gather.2.cloned.1.call-update
  11.4 0.0 copy-done.16
  11.4 0.2 convert_reduce_fusion
  11.6 0.0 copy-done.17
  11.7 0.0 copy-done.18
  11.7 0.2 select_reduce_fusion
  11.8 0.1 convert_element_type.31
  12.0 1.3 copy-done.2
  13.3 0.0 copy-done.9
  13.3 2.8 copy-done.3
  16.1 12.7 %messages.1 = (bf16[32,1168,128]{2,1,0:T(8,128)(2,1)}, bf16[32,384,128]{2,1,0:T(8,128)(2,1)S(1)}) custom-call(s32[384]{0:T(512)S(1)} %get-tuple-element.64.tile_ids, s32[384]{0:T(512)S(1)} %get-tuple-element.63.row_ids, bf16[12288,128]{1,0:T(8,128)(2,1)S(1)} %copy-done.2, s32[1,12288]{1,0:T(1,128)S(1)} %bitcast.13, bf16[192,128,128]{2,1,0:T(8,128)(2,1)S(1)} %copy-done.3, ...), custom_call_target="tpu_custom_call" | custom-call | flops 1610612 | bytes 22020 | tf_op jit(solution)/shard_map/messages/pallas_call | solution.py:77
  28.9 118.3 %all_to_all.20.received = bf16[32,1168,128]{2,1,0:T(8,128)(2,1)S(1)} all-to-all(bf16[32,1168,128]{2,1,0:T(8,128)(2,1)} %get-tuple-element.36), channel_id=1, replica_groups=mesh['dom'=32,'hid'=4] {'dom'}, dimensions={0} | all-to-all | bytes 19136512 | tf_op jit(solution)/shard_map/all_to_all | solution.py:294
  147.2 0.0 copy-done.4
  147.2 0.1 fusion.1
  147.2 0.0 copy-start
  147.2 3.6 %copy-done = bf16[32,1168,128]{2,1,0:T(8,128)(2,1)} copy-done((bf16[32,1168,128]{2,1,0:T(8,128)(2,1)}, bf16[32,1168,128]{2,1,0:T(8,128)(2,1)S(1)}, u32[]{:S(2)}) %copy-start) | copy-done | bytes 9568280
  150.9 0.1 reshape.59.col_ids
  151.0 3.7 %copy-done.1 = bf16[32,1168,128]{2,1,0:T(8,128)(2,1)S(1)} copy-done((bf16[32,1168,128]{2,1,0:T(8,128)(2,1)S(1)}, bf16[32,1168,128]{2,1,0:T(8,128)(2,1)}, u32[]{:S(2)}) %copy-start.1) | copy-done | bytes 9568280
  154.7 5.1 %unit_sums.2 = (bf16[144,3072]{1,0:T(8,128)(2,1)S(1)}, bf16[144,3072]{1,0:T(8,128)(2,1)S(1)}, bf16[144,3072]{1,0:T(8,128)(2,1)S(1)}, bf16[144,3072]{1,0:T(8,128)(2,1)S(1)}) custom-call(s32[384]{0:T(512)S(1)} %reshape.59.col_ids, s32[1]{0:T(128)} %bitcast.2.place, bf16[32,1168,128]{2,1,0:T(8,128)(2,1)S(1)} %copy-done.1, ...), custom_call_target="tpu_custom_call" | custom-call | flops 4718 | bytes 9437 | tf_op jit(solution)/shard_map/unit_sums/pallas_call | solution.py:132
  159.8 1.0 copy-done.7
  160.8 0.9 copy-done.10
  161.7 0.9 copy-done.11
  162.6 0.9 copy-done.12
  163.5 4.6 %all-to-all-start.1 = ((bf16[32,384,128]{2,1,0:T(8,128)(2,1)}), bf16[32,384,128]{2,1,0:T(8,128)(2,1)S(1)}, u32[]{:S(2)}, u32[]{:S(2)}) async-start(bf16[32,384,128]{2,1,0:T(8,128)(2,1)} %copy-done.4), calls=%async_computation.1 | async-start | bytes 6291456 | tf_op jit(solution)/shard_map/all_to_all | solution.py:294
  168.1 1.4 collective-permute-start
  169.5 2.6 collective-permute-start.1
  172.1 1.1 collective-permute-start.2
  173.1 34.2 %all-to-all-done.1.received = bf16[32,384,128]{2,1,0:T(8,128)(2,1)S(1)} async-done(((bf16[32,384,128]{2,1,0:T(8,128)(2,1)}), bf16[32,384,128]{2,1,0:T(8,128)(2,1)S(1)}, u32[]{:S(2)}, u32[]{:S(2)}) %all-to-all-start.1) | async-done | bytes 3145760 | tf_op jit(solution)/shard_map/all_to_all | solution.py:294
  207.3 3.2 %unit_sums.3 = (bf16[32,3072]{1,0:T(8,128)(2,1)S(1)}, bf16[32,3072]{1,0:T(8,128)(2,1)S(1)}, bf16[32,3072]{1,0:T(8,128)(2,1)S(1)}, bf16[32,3072]{1,0:T(8,128)(2,1)S(1)}) custom-call(s32[384]{0:T(512)S(1)} %reshape.59.col_ids, s32[1]{0:T(128)} %bitcast.2.place, bf16[32,384,128]{2,1,0:T(8,128)(2,1)S(1)} %all-to-all-done.1.received), custom_call_target="tpu_custom_call" | custom-call | flops 1572 | bytes 9437 | tf_op jit(solution)/shard_map/unit_sums/pallas_call | solution.py:132
  210.5 1.4 collective-permute-start.3
  211.9 2.6 collective-permute-start.4
  214.5 0.0 collective-permute-done.rest_1_
  214.5 1.1 collective-permute-start.5
  215.6 1.9 copy-done.6
  217.5 10.1 %weight_parts.1 = f32[32,40,128]{2,1,0:T(8,128)} custom-call(s32[1]{0:T(128)} %bitcast.2.place, bf16[12288,128]{1,0:T(8,128)(2,1)S(1)} %copy-done.5, bf16[12288,128]{1,0:T(8,128)(2,1)S(1)} %copy-done.6, bf16[12288,512]{1,0:T(8,128)(2,1)} %all-gather.2.cloned.1.call-done.grad.rest_8_), custom_call_target="tpu_custom_call" | custom-call | flops 3221225 | bytes 19922 | tf_op jit(solution)/shard_map/weight_parts/pallas_call | solution.py:241
  227.5 0.0 collective-permute-done.1.rest_2_
  227.6 0.0 collective-permute-done.2.rest_3_
  227.6 0.0 collective-permute-done.3.rest_5_
  227.6 0.0 collective-permute-done.4.rest_6_
  227.6 0.0 collective-permute-done.5.rest_7_
  227.6 0.0 copy-done.8
  227.6 7.1 %turn.1 = (bf16[3072,128]{1,0:T(8,128)(2,1)S(1)}, bf16[3072,128]{1,0:T(8,128)(2,1)}, bf16[3072,128]{1,0:T(8,128)(2,1)}, bf16[3072,128]{1,0:T(8,128)(2,1)S(1)}) custom-call(s32[1]{0:T(128)} %bitcast.2.place, bf16[144,3072]{1,0:T(8,128)(2,1)S(1)} %copy-done.8, bf16[144,3072]{1,0:T(8,128)(2,1)} %collective-permute-done.rest_1_, ...), custom_call_target="tpu_custom_call" | custom-call | flops 3221225 | bytes 10485 | tf_op jit(solution)/shard_map/turn/pallas_call | solution.py:193
  234.7 0.9 copy-done.13
  235.6 7.8 %all-to-all-start.2 = ((f32[32,40,128]{2,1,0:T(8,128)}), f32[32,40,128]{2,1,0:T(8,128)}, u32[]{:S(2)}, u32[]{:S(2)}) async-start(f32[32,40,128]{2,1,0:T(8,128)} %weight_parts.1), calls=%async_computation.2 | async-start | bytes 1310720 | tf_op jit(solution)/shard_map/all_to_all | solution.py:294
  243.3 0.5 collective-permute-start.6
  243.8 0.5 collective-permute-start.7
  244.3 2.0 collective-permute-start.8
  246.3 10.1 %all-to-all-done.2 = f32[32,40,128]{2,1,0:T(8,128)} async-done(((f32[32,40,128]{2,1,0:T(8,128)}), f32[32,40,128]{2,1,0:T(8,128)}, u32[]{:S(2)}, u32[]{:S(2)}) %all-to-all-start.2) | async-done | bytes 655392 | tf_op jit(solution)/shard_map/all_to_all | solution.py:294
  256.4 1.1 reduce_sum.49
  257.6 0.9 broadcast_in_dim.38
  258.4 4.7 %all-to-all-start.3 = ((f32[32,32,128]{2,1,0:T(8,128)}), f32[32,32,128]{2,1,0:T(8,128)}, u32[]{:S(2)}, u32[]{:S(2)}) async-start(f32[32,32,128]{2,1,0:T(8,128)} %broadcast_in_dim.38), calls=%async_computation.3 | async-start | bytes 1048576 | tf_op jit(solution)/shard_map/all_to_all | solution.py:294
  263.2 0.5 fusion.2
  263.7 16.7 %collective-permute-done.6.rest_1_ = bf16[3072,128]{1,0:T(8,128)(2,1)S(1)} collective-permute-done((bf16[3072,128]{1,0:T(8,128)(2,1)}, bf16[3072,128]{1,0:T(8,128)(2,1)S(1)}, u32[]{:S(2)}, u32[]{:S(2)}) %collective-permute-start.6) | collective-permute-done | bytes 786464 | tf_op jit(solution)/shard_map/ppermute | solution.py:289
  280.4 0.0 collective-permute-done.7.rest_2_
  280.4 0.3 collective-permute-done.8.rest_3_
  280.7 2.1 place_quarters.1
  282.9 0.0 all-to-all-done.3
  282.9 1.1 multiply_bitcast_fusion
  284.0 0.8 slice_bitcast_fusion
  (24 shorter events, 0.1 us)
Async XLA Ops:
  7.2 156.4 %all-gather.2.cloned.1.call-start = ((), (), s32[]{:S(2)}) async-start(), calls=%async_computation.4 | async-start | bytes 15728640 | tf_op jit(solution)/shard_map/all_gather | solution.py:321
  7.2 4.2 %copy-start.16 = (s32[192,1]{0,1:T(1,128)S(1)}, s32[192,1]{0,1:T(1,128)}, u32[]{:S(2)}) copy-start(s32[192,1]{0,1:T(1,128)} %param.20) | copy-start | bytes 2308
  7.2 4.4 %copy-start.17 = (s32[192]{0:T(256)S(1)}, s32[192]{0:T(256)}, u32[]{:S(2)}) copy-start(s32[192]{0:T(256)} %param.19) | copy-start | bytes 2308
  7.2 4.4 %copy-start.18 = (s32[192]{0:T(256)S(1)}, s32[192]{0:T(256)}, u32[]{:S(2)}) copy-start(s32[192]{0:T(256)} %param.18) | copy-start | bytes 2308
  11.4 1.9 copy-start.2
  11.4 1.9 copy-start.9
  13.3 2.8 copy-start.3
  16.1 12.7 %copy-start.14 = (bf16[128,512]{1,0:T(8,128)(2,1)S(1)}, bf16[128,512]{1,0:T(8,128)(2,1)}, u32[]{:S(2)}) copy-start(bf16[128,512]{1,0:T(8,128)(2,1)} %param.15) | copy-start | bytes 393220
  16.1 12.7 %copy-start.15 = (bf16[128,512]{1,0:T(8,128)(2,1)S(1)}, bf16[128,512]{1,0:T(8,128)(2,1)}, u32[]{:S(2)}) copy-start(bf16[128,512]{1,0:T(8,128)(2,1)} %param.16) | copy-start | bytes 393220
  28.8 118.3 %copy-start.4 = (bf16[32,384,128]{2,1,0:T(8,128)(2,1)}, bf16[32,384,128]{2,1,0:T(8,128)(2,1)S(1)}, u32[]{:S(2)}) copy-start(bf16[32,384,128]{2,1,0:T(8,128)(2,1)S(1)} %get-tuple-element.48) | copy-start | bytes 9437188
  147.2 3.6 %copy-start = (bf16[32,1168,128]{2,1,0:T(8,128)(2,1)}, bf16[32,1168,128]{2,1,0:T(8,128)(2,1)S(1)}, u32[]{:S(2)}) copy-start(bf16[32,1168,128]{2,1,0:T(8,128)(2,1)S(1)} %all_to_all.20.received) | copy-start | bytes 28704772
  151.0 3.7 %copy-start.1 = (bf16[32,1168,128]{2,1,0:T(8,128)(2,1)S(1)}, bf16[32,1168,128]{2,1,0:T(8,128)(2,1)}, u32[]{:S(2)}) copy-start(bf16[32,1168,128]{2,1,0:T(8,128)(2,1)} %copy-done) | copy-start | bytes 28704772
  159.8 1.0 copy-start.7
  160.8 0.9 copy-start.10
  161.7 0.9 copy-start.11
  162.6 0.9 copy-start.12
  163.5 43.8 %all-to-all-start.1 = ((bf16[32,384,128]{2,1,0:T(8,128)(2,1)}), bf16[32,384,128]{2,1,0:T(8,128)(2,1)S(1)}, u32[]{:S(2)}, u32[]{:S(2)}) async-start(bf16[32,384,128]{2,1,0:T(8,128)(2,1)} %copy-done.4), calls=%async_computation.1 | async-start | bytes 6291456 | tf_op jit(solution)/shard_map/all_to_all | solution.py:294
  168.1 46.4 %collective-permute-start = (bf16[144,3072]{1,0:T(8,128)(2,1)}, bf16[144,3072]{1,0:T(8,128)(2,1)}, u32[]{:S(2)}, u32[]{:S(2)}) collective-permute-start(bf16[144,3072]{1,0:T(8,128)(2,1)} %copy-done.12), channel_id=1, source_target_pairs={{0,1},{1,2},{2,3},{3,0},{4,5},{5,6},{6,7},{7,4},{8,9},{9,10},{10,1... | collective-permute-start | bytes 2654216 | tf_op jit(solution)/shard_map/ppermute | solution.py:289
  169.5 58.1 %collective-permute-start.1 = (bf16[144,3072]{1,0:T(8,128)(2,1)}, bf16[144,3072]{1,0:T(8,128)(2,1)}, u32[]{:S(2)}, u32[]{:S(2)}) collective-permute-start(bf16[144,3072]{1,0:T(8,128)(2,1)} %copy-done.11), channel_id=1, source_target_pairs={{0,2},{1,3},{2,0},{3,1},{4,6},{5,7},{6,4},{7,5},{8,10},{9,11},{10,... | collective-permute-start | bytes 2654216 | tf_op jit(solution)/shard_map/ppermute | solution.py:289
  172.1 55.5 %collective-permute-start.2 = (bf16[144,3072]{1,0:T(8,128)(2,1)}, bf16[144,3072]{1,0:T(8,128)(2,1)}, u32[]{:S(2)}, u32[]{:S(2)}) collective-permute-start(bf16[144,3072]{1,0:T(8,128)(2,1)} %copy-done.10), channel_id=1, source_target_pairs={{0,3},{1,0},{2,1},{3,2},{4,7},{5,4},{6,5},{7,6},{8,11},{9,8},{10,9... | collective-permute-start | bytes 2654216 | tf_op jit(solution)/shard_map/ppermute | solution.py:289
  207.3 8.3 %copy-start.5 = (bf16[12288,128]{1,0:T(8,128)(2,1)S(1)}, bf16[12288,128]{1,0:T(8,128)(2,1)}, u32[]{:S(2)}) copy-start(bf16[12288,128]{1,0:T(8,128)(2,1)} %first.1) | copy-start | bytes 9437188
  210.5 17.0 %collective-permute-start.3 = (bf16[32,3072]{1,0:T(8,128)(2,1)S(1)}, bf16[32,3072]{1,0:T(8,128)(2,1)S(1)}, u32[]{:S(2)}, u32[]{:S(2)}) collective-permute-start(bf16[32,3072]{1,0:T(8,128)(2,1)S(1)} %get-tuple-element.50), channel_id=1, source_target_pairs={{0,1},{1,2},{2,3},{3,0},{4,5},{5,6},{6,7},{7,4},{8,9},{9,10},{10,1... | collective-permute-start | bytes 589832 | tf_op jit(solution)/shard_map/ppermute | solution.py:289
  211.9 15.7 %collective-permute-start.4 = (bf16[32,3072]{1,0:T(8,128)(2,1)S(1)}, bf16[32,3072]{1,0:T(8,128)(2,1)S(1)}, u32[]{:S(2)}, u32[]{:S(2)}) collective-permute-start(bf16[32,3072]{1,0:T(8,128)(2,1)S(1)} %get-tuple-element.51), channel_id=1, source_target_pairs={{0,2},{1,3},{2,0},{3,1},{4,6},{5,7},{6,4},{7,5},{8,10},{9,11},{10,... | collective-permute-start | bytes 589832 | tf_op jit(solution)/shard_map/ppermute | solution.py:289
  214.5 13.1 %collective-permute-start.5 = (bf16[32,3072]{1,0:T(8,128)(2,1)S(1)}, bf16[32,3072]{1,0:T(8,128)(2,1)S(1)}, u32[]{:S(2)}, u32[]{:S(2)}) collective-permute-start(bf16[32,3072]{1,0:T(8,128)(2,1)S(1)} %get-tuple-element.52), channel_id=1, source_target_pairs={{0,3},{1,0},{2,1},{3,2},{4,7},{5,4},{6,5},{7,6},{8,11},{9,8},{10,9... | collective-permute-start | bytes 589832 | tf_op jit(solution)/shard_map/ppermute | solution.py:289
  215.6 1.9 copy-start.6
  217.4 10.1 %copy-start.8 = (bf16[144,3072]{1,0:T(8,128)(2,1)S(1)}, bf16[144,3072]{1,0:T(8,128)(2,1)}, u32[]{:S(2)}) copy-start(bf16[144,3072]{1,0:T(8,128)(2,1)} %copy-done.7) | copy-start | bytes 2654212
  234.7 0.9 copy-start.13
  235.6 20.8 %all-to-all-start.2 = ((f32[32,40,128]{2,1,0:T(8,128)}), f32[32,40,128]{2,1,0:T(8,128)}, u32[]{:S(2)}, u32[]{:S(2)}) async-start(f32[32,40,128]{2,1,0:T(8,128)} %weight_parts.1), calls=%async_computation.2 | async-start | bytes 1310720 | tf_op jit(solution)/shard_map/all_to_all | solution.py:294
  243.3 37.0 %collective-permute-start.6 = (bf16[3072,128]{1,0:T(8,128)(2,1)}, bf16[3072,128]{1,0:T(8,128)(2,1)S(1)}, u32[]{:S(2)}, u32[]{:S(2)}) collective-permute-start(bf16[3072,128]{1,0:T(8,128)(2,1)} %get-tuple-element.58), channel_id=1, source_target_pairs={{0,1},{1,2},{2,3},{3,0},{4,5},{5,6},{6,7},{7,4},{8,9},{9,10},{10,1... | collective-permute-start | bytes 2359304 | tf_op jit(solution)/shard_map/ppermute | solution.py:289
  243.8 36.6 %collective-permute-start.7 = (bf16[3072,128]{1,0:T(8,128)(2,1)}, bf16[3072,128]{1,0:T(8,128)(2,1)S(1)}, u32[]{:S(2)}, u32[]{:S(2)}) collective-permute-start(bf16[3072,128]{1,0:T(8,128)(2,1)} %get-tuple-element.59), channel_id=1, source_target_pairs={{0,2},{1,3},{2,0},{3,1},{4,6},{5,7},{6,4},{7,5},{8,10},{9,11},{10,... | collective-permute-start | bytes 2359304 | tf_op jit(solution)/shard_map/ppermute | solution.py:289
  244.3 36.4 %collective-permute-start.8 = (bf16[3072,128]{1,0:T(8,128)(2,1)}, bf16[3072,128]{1,0:T(8,128)(2,1)S(1)}, u32[]{:S(2)}, u32[]{:S(2)}) collective-permute-start(bf16[3072,128]{1,0:T(8,128)(2,1)} %copy-done.13), channel_id=1, source_target_pairs={{0,3},{1,0},{2,1},{3,2},{4,7},{5,4},{6,5},{7,6},{8,11},{9,8},{10,9... | collective-permute-start | bytes 2359304 | tf_op jit(solution)/shard_map/ppermute | solution.py:289
  258.4 24.5 %all-to-all-start.3 = ((f32[32,32,128]{2,1,0:T(8,128)}), f32[32,32,128]{2,1,0:T(8,128)}, u32[]{:S(2)}, u32[]{:S(2)}) async-start(f32[32,32,128]{2,1,0:T(8,128)} %broadcast_in_dim.38), calls=%async_computation.3 | async-start | bytes 1048576 | tf_op jit(solution)/shard_map/all_to_all | solution.py:294
Sparse Core Ops, SparseCore 0:
  11.6 125.2 all-gather.1

commit v2 on v1

--- a/solution.py
+++ b/solution.py
@@ -14,16 +14,14 @@
 TAIL = BLK - HEAD
 MARK = 16
 CHUNK = 2048
-WROWS = 48
 GROUP = 8
-SLICES = 3
-VMEM = 40 * 1024 * 1024
+SLICES = 2
 F32, BF16 = jnp.float32, jnp.bfloat16
 
 
-def params():
+def params(limit=40):
     return pltpu.CompilerParams(
-        dimension_semantics=("arbitrary",), vmem_limit_bytes=VMEM
+        dimension_semantics=("arbitrary",), vmem_limit_bytes=limit * 1024 * 1024
     )
 
 
@@ -35,13 +33,61 @@
     return pl.ds(pl.multiple_of(start, BLK), size)
 
 
-def message_kernel(tile_ids, row_ids, grad, degree, far, cols, head, tail, rows, tiles, sem):
+def mask_kernel(pre_relu, grad_out, near, own, out):
     step = pl.program_id(0)
 
+    @pl.when(step < pl.num_programs(0) - 1)
+    def _():
+        out[...] = jnp.where(pre_relu[...] > 0, grad_out[...], jnp.zeros_like(grad_out))
+
+    @pl.when(step == pl.num_programs(0) - 1)
+    def _():
+        count = near.shape[1] // BLK
+        for i, weight in enumerate((near, own)):
+            for q in range(count):
+                at = (i * count + q) * BLK
+                out[at : at + BLK, :] = weight[:, q * BLK : (q + 1) * BLK]
+
+
+def masked(pre_relu, grad_out, near, own):
+    hosts = grad_out.shape[0]
+    extra = 2 * near.shape[1]
+    chunk = 2 * extra
+    steps = hosts // chunk
+    whole = pl.BlockSpec(memory_space=pltpu.VMEM)
+    piece = pl.BlockSpec((chunk, BLK), lambda i: (jnp.minimum(i, steps - 1), 0))
+    return pl.pallas_call(
+        mask_kernel,
+        grid=(steps + 1,),
+        in_specs=[piece, piece, whole, whole],
+        out_specs=pl.BlockSpec((chunk, BLK), lambda i: (i, 0)),
+        out_shape=jax.ShapeDtypeStruct((hosts + extra, BLK), BF16),
+        compiler_params=params(60),
+        cost_estimate=cost(0, 9 << 20),
+        name="masked",
+    )(pre_relu, grad_out, near, own)
+
+
+def message_kernel(
+    tile_ids, row_ids, far_grad, degree, far_tiles, cols, head, tail, rows, tiles, grad, sems
+):
+    step = pl.program_id(0)
+    pieces = sems.shape[0] - 1
+    width = grad.shape[0] // pieces
+
     @pl.when(step == 0)
     def _():
-        fetch = pltpu.make_async_copy(far, tiles, sem)
-        fetch.start()
+        fetches = [
+            pltpu.make_async_copy(
+                far_grad.at[pl.ds(i * width, width), :],
+                grad.at[pl.ds(i * width, width), :],
+                sems.at[i],
+            )
+            for i in range(pieces)
+        ]
+        fetches.append(pltpu.make_async_copy(far_tiles, tiles, sems.at[pieces]))
+        for fetch in fetches:
+            fetch.start()
 
         def turn(b, carry):
             at = lanes(b * BLK, BLK)
@@ -49,8 +95,11 @@
             rows[:, at] = (turned * (1.0 / degree[:, at].astype(F32))).astype(BF16)
             return carry
 
-        lax.fori_loop(0, grad.shape[0] // BLK, turn, 0, unroll=8)
-        fetch.wait()
+        blocks = width // BLK
+        for i in range(pieces):
+            fetches[i].wait()
+            lax.fori_loop(i * blocks, (i + 1) * blocks, turn, 0, unroll=8)
+        fetches[pieces].wait()
 
     def one(g, carry):
         base = (step * GROUP + g) * CAP
@@ -67,8 +116,9 @@
 
 
 def messages(tile_ids, row_ids, grad, degree, tiles, cols):
-    owners, hosts = cols.shape[0], grad.shape[0]
+    owners, hosts = cols.shape[0], degree.shape[1]
     whole = pl.BlockSpec(memory_space=pltpu.VMEM)
+    far = pl.BlockSpec(memory_space=pltpu.HBM)
 
     def group(height):
         return pl.BlockSpec((GROUP, height, BLK), lambda o, *_: (o, 0, 0))
@@ -79,77 +129,114 @@
         grid_spec=pltpu.PrefetchScalarGridSpec(
             num_scalar_prefetch=2,
             grid=(owners // GROUP,),
-            in_specs=[whole, whole, pl.BlockSpec(memory_space=pl.ANY), group(MARK)],
+            in_specs=[far, whole, far, group(MARK)],
             out_specs=[group(h) for h in heights],
             scratch_shapes=[
                 pltpu.VMEM((BLK, hosts), BF16),
                 pltpu.VMEM(tiles.shape, BF16),
-                pltpu.SemaphoreType.DMA,
+                pltpu.VMEM((hosts, BLK), BF16),
+                pltpu.SemaphoreType.DMA((5,)),
             ],
         ),
         out_shape=[jax.ShapeDtypeStruct((owners, h, BLK), BF16) for h in heights],
-        compiler_params=params(),
+        compiler_params=params(60),
         cost_estimate=cost(2 * owners * CAP * BLK**3, 21 << 20),
         name="messages",
     )(tile_ids, row_ids, grad, degree, tiles, cols)
 
 
-def sum_kernel(height, parts, col_ids, place, received, *rest):
-    weights, outs, total = rest[: -parts - 1], rest[-parts - 1 : -1], rest[-1]
-    step = pl.program_id(0)
-
-    @pl.when(step == 0)
-    def _():
-        total[...] = jnp.zeros_like(total)
-
-    def one(g, carry):
-        base = (step * GROUP + g) * CAP
-        for k in range(CAP):
-            at = lanes(col_ids[base + k] * BLK, BLK)
-            total[:, at] += received[g, k * height : (k + 1) * height, :].astype(F32)
-        return carry
-
-    lax.fori_loop(0, GROUP, one, 0)
-
-    @pl.when(step == pl.num_programs(0) - 1)
-    def _():
-        width = outs[0].shape[1]
-        for k, out in enumerate(outs):
-            to = lax.rem(place[0] + k, parts)
-            out[:height, :] = total[:, lanes(to * width, width)].astype(BF16)
-            for weight in weights:
-                units = weight.shape[1]
-                for i, r in enumerate(range(0, weight.shape[0], WROWS)):
-                    piece = weight[r : r + WROWS, :]
-                    out[height : height + piece.shape[0], i * units : (i + 1) * units] = piece
-
-
-def unit_sums(height, col_ids, place, received, blocks, parts, weight=None):
+def sum_kernel(height, place, received, *rest):
+    parts = 4
+    first = height == HEAD
+    if not first:
+        sent_marks, rest = rest[0], rest[1:]
+    outs, rest = rest[:parts], rest[parts:]
+    if first:
+        marks, total, held, ready, cols, col_sem, in_sems, out_sems, marked = rest
+    else:
+        total, held, ready, cols, col_sem, in_sems, out_sems = rest
+    groups = received.shape[0] // GROUP
+
+    def fetch(g):
+        source = received.at[pl.ds(g * GROUP, GROUP), pl.ds(0, CAP * height), :]
+        return pltpu.make_async_copy(source, held.at[g % 2], in_sems.at[g % 2])
+
+    if first:
+        source = received.at[:, pl.ds(CAP * HEAD, MARK), :]
+        copy = pltpu.make_async_copy(source, marked, col_sem)
+        copy.start()
+        fetch(0).start()
+        copy.wait()
+        marks[...] = marked[:, 0, :].astype(F32).astype(jnp.int32)
+        copy = pltpu.make_async_copy(marks, cols, col_sem)
+        copy.start()
+    else:
+        copy = pltpu.make_async_copy(sent_marks, cols, col_sem)
+        copy.start()
+        fetch(0).start()
+    total[...] = jnp.zeros_like(total)
+    copy.wait()
+    for g in range(groups):
+        if g + 1 < groups:
+            fetch(g + 1).start()
+        fetch(g).wait()
+
+        def one(i, carry, g=g):
+            for k in range(CAP):
+                at = lanes(cols[g * GROUP + i, k] * BLK, BLK)
+                total[:, at] += held[g % 2, i, k * height : (k + 1) * height, :].astype(F32)
+            return carry
+
+        lax.fori_loop(0, GROUP, one, 0)
+
+    width = ready.shape[2]
+    copies = []
+    for k, out in enumerate(outs):
+        to = lax.rem(place[0] + k, parts)
+        ready[k, :, :] = total[:, lanes(to * width, width)].astype(BF16)
+        copies.append(pltpu.make_async_copy(ready.at[k], out, out_sems.at[k]))
+        copies[k].start()
+    for copy in copies:
+        copy.wait()
+
+
+def unit_sums(height, place, received, blocks, parts, *sent_marks):
+    first = height == HEAD
     sources = received.shape[0]
     width = blocks * BLK // parts
-    extra = [] if weight is None else [weight]
-    shape = (height + WROWS * len(extra), width)
-    return pl.pallas_call(
-        functools.partial(sum_kernel, height, parts),
+    shape = (height, width)
+    far = pl.BlockSpec(memory_space=pltpu.HBM)
+    near = pl.BlockSpec(memory_space=pltpu.VMEM)
+    marks = jax.ShapeDtypeStruct((sources, BLK), jnp.int32)
+    return pl.pallas_call(
+        functools.partial(sum_kernel, height),
         grid_spec=pltpu.PrefetchScalarGridSpec(
-            num_scalar_prefetch=2,
-            grid=(sources // GROUP,),
-            in_specs=[pl.BlockSpec((GROUP, CAP * height, BLK), lambda p, *_: (p, 0, 0))]
-            + [pl.BlockSpec(memory_space=pltpu.VMEM)] * len(extra),
-            out_specs=[pl.BlockSpec(shape, lambda p, *_: (0, 0))] * parts,
-            scratch_shapes=[pltpu.VMEM((height, (blocks + 1) * BLK), F32)],
-        ),
-        out_shape=[jax.ShapeDtypeStruct(shape, BF16)] * parts,
-        compiler_params=params(),
+            num_scalar_prefetch=1,
+            grid=(1,),
+            in_specs=[far] + [near] * len(sent_marks),
+            out_specs=[far] * parts + [near] * first,
+            scratch_shapes=[
+                pltpu.VMEM((height, (blocks + 1) * BLK), F32),
+                pltpu.VMEM((2, GROUP, CAP * height, BLK), BF16),
+                pltpu.VMEM((parts,) + shape, BF16),
+                pltpu.SMEM(marks.shape, jnp.int32),
+                pltpu.SemaphoreType.DMA,
+                pltpu.SemaphoreType.DMA((2,)),
+                pltpu.SemaphoreType.DMA((parts,)),
+            ]
+            + [pltpu.VMEM((sources, MARK, BLK), BF16)] * first,
+        ),
+        out_shape=[jax.ShapeDtypeStruct(shape, BF16)] * parts + [marks] * first,
+        compiler_params=params(53 if first else 40),
         cost_estimate=cost(sources * CAP * height * BLK, 9 << 20),
         name="unit_sums",
-    )(col_ids, place, received, *extra)
+    )(place, received, *sent_marks)
 
 
 def turn_kernel(place, *rest):
-    parts = (len(rest) - 3) // 3
-    heads, tails, grad = rest[:parts], rest[parts : 2 * parts], rest[2 * parts]
-    outs, near, own = rest[2 * parts + 1 : -2], rest[-2], rest[-1]
+    parts = (len(rest) - 4) // 3
+    heads, tails, (grad, weights) = rest[:parts], rest[parts : 2 * parts], rest[2 * parts :][:2]
+    outs, near, own = rest[2 * parts + 2 : -2], rest[-2], rest[-1]
     units = grad.shape[1]
     chunk = outs[0].shape[0]
     step = pl.program_id(0)
@@ -157,27 +244,18 @@
     @pl.when(step == 0)
     def _():
         for k in range(parts):
-            sender = heads[(parts - k) % parts]
-            rows = [
-                sender[HEAD : HEAD + min(WROWS, 2 * BLK - r), i * units : (i + 1) * units]
-                for i, r in enumerate(range(0, 2 * BLK, WROWS))
-            ]
-            both = jnp.concatenate(rows, axis=0)
-            own[:, k * BLK : (k + 1) * BLK] = both[BLK:].T
-            near[k * BLK : (k + 1) * BLK, :] = both[:BLK]
-
-        for k in range(parts):
-            rows = slice(k * BLK, (k + 1) * BLK)
-            blocks = [
-                near[rows, lanes(lax.rem(place[0] + parts - i, parts) * BLK, BLK)]
-                for i in range(parts)
-            ]
-            near[rows, :] = jnp.concatenate(blocks, axis=1)
+            to = lanes(lax.rem(place[0] + k, parts) * BLK, BLK)
+            here = slice(k * BLK, (k + 1) * BLK)
+            for i in range(parts):
+                sender = lax.rem(place[0] + parts - i, parts) * BLK
+                part = slice(i * BLK, (i + 1) * BLK)
+                near[here, part] = weights[lanes(sender, BLK), to]
+                own[part, here] = weights[units + i * BLK : units + (i + 1) * BLK, to].T
 
     at = lanes(step * chunk, chunk)
     sums = []
     for head, tail in zip(heads, tails):
-        sums += [head[:HEAD, at], tail[:, at]]
+        sums += [head[:, at], tail[:, at]]
     turned = jnp.dot(near[...], jnp.concatenate(sums, axis=0), preferred_element_type=F32)
     result = jnp.dot(grad[...], own[...], preferred_element_type=F32)
     for k, out in enumerate(outs):
@@ -189,6 +267,7 @@
     parts, width = len(heads), tails[0].shape[1]
     units = grad.shape[1]
     chunk = width // SLICES
+    last = grad.shape[0] // (2 * units) - 1
     whole = pl.BlockSpec(memory_space=pltpu.VMEM)
     return pl.pallas_call(
         turn_kernel,
@@ -196,7 +275,10 @@
             num_scalar_prefetch=1,
             grid=(SLICES,),
             in_specs=[whole] * (2 * parts)
-            + [pl.BlockSpec((chunk, units), lambda i, place: (place[0] * SLICES + i, 0))],
+            + [
+                pl.BlockSpec((chunk, units), lambda i, place: (place[0] * SLICES + i, 0)),
+                pl.BlockSpec((2 * units, units), lambda i, *_: (last, 0)),
+            ],
             out_specs=[pl.BlockSpec((chunk, BLK), lambda i, *_: (i, 0))] * parts,
             scratch_shapes=[pltpu.VMEM((units, units), BF16)] * 2,
         ),
@@ -204,7 +286,7 @@
         compiler_params=params(),
         cost_estimate=cost(4 * units * units * width, 10 << 20),
         name="turn",
-    )(place, *heads, *tails, grad)
+    )(place, *heads, *tails, grad, grad)
 
 
 def weight_kernel(place, first, second, grad, out, total, bias):
@@ -235,7 +317,7 @@
 
 
 def weight_parts(place, first, second, grad, owners):
-    hosts, units = grad.shape
+    hosts, units = first.shape[0], grad.shape[1]
     height = 8 * (units // BLK) + 8
     piece = pl.BlockSpec((CHUNK, BLK), lambda i, *_: (i, 0))
     return pl.pallas_call(
@@ -317,7 +399,7 @@
     place = lax.axis_index("hid").astype(jnp.int32).reshape(1)
     degree = in_degree.reshape(1, hosts)
 
-    grad = jnp.where(pre_relu > 0, grad_out, jnp.zeros_like(grad_out))
+    grad = masked(pre_relu, grad_out, w_neigh, w_self)
     full_grad = lax.all_gather(grad, "hid", axis=1, tiled=True)
 
     owner = tile_owner[:, 0]
@@ -333,26 +415,26 @@
     )
 
     head, tail = messages(tile_ids, row_ids, grad, degree, adj_tiles, cols)
-    weights = jnp.concatenate([w_neigh, w_self], axis=0)
-    head, tail, place, weights = lax.optimization_barrier((head, tail, place, weights))
-    head = swap(head)
-    col_ids = head[:, CAP * HEAD, :CAP].astype(jnp.int32).reshape(slots)
-    heads = unit_sums(HEAD, col_ids, place, head, blocks, parts, weights)
-    heads, tail, full_grad = lax.optimization_barrier((heads, tail, full_grad))
+    head, tail, place = lax.optimization_barrier((head, tail, place))
+    head, tail = lax.optimization_barrier((swap(head), tail))
+    tail = swap(tail)
+    *heads, marks = unit_sums(HEAD, place, head, blocks, parts)
+    heads, full_grad = lax.optimization_barrier((heads, full_grad))
     heads = exchange(heads)
-    tails = unit_sums(TAIL, col_ids, place, swap(tail), blocks, parts)
-    tails = exchange(tails)
-
     pieces = weight_parts(place, features, neigh_mean, full_grad, owners)
-    quarters = turn(place, heads, tails, full_grad)
+    tail, pieces, heads = lax.optimization_barrier((tail, pieces, heads))
+    tails = unit_sums(TAIL, place, tail, blocks, parts, marks)
+    quarters = turn(place, heads, exchange(tails), full_grad)
     pieces, quarters = lax.optimization_barrier((pieces, quarters))
     quarters = exchange(quarters)
     summed = jnp.sum(swap(pieces), axis=0)
     rows = 8 * parts
+    summed, quarters[2] = lax.optimization_barrier((summed, quarters[2]))
     gathered = swap(jnp.broadcast_to(summed[:rows], (owners, rows, BLK)))
     grads = gathered.reshape(owners, parts, 8, BLK).transpose(0, 2, 1, 3)
     grads = grads.reshape(2 * BLK, parts * BLK) * scale
     bias = summed[rows] * scale
+    quarters, grads, bias = lax.optimization_barrier((quarters, grads, bias))
 
     return place_quarters(place, quarters), grads[:BLK], grads[BLK:], bias
 

time: 292 us -> 274 us (0.938)
  waiting for transfers between devices: 61.4 us -> 37.8 us
  Pallas kernels: 40.4 us -> 54.2 us
  local copies, waits for them, and re-layouts: 19.9 us -> 8.62 us
  starting transfers between devices: 30.1 us -> 36.3 us
  other arithmetic: 7.34 us -> 3.7 us
    unnamed x38 -> x16, local copies, waits for them, and re-layouts: 18 us -> 6.13 us
    all_to_all x3, waiting for transfers between devices: 44.3 us -> 32.5 us  [swap(): return lax.all_to_all(array, 'dom', split_axis=0, concat_axis=0, tiled=True)]
    ppermute x9, waiting for transfers between devices: 17.1 us -> 5.33 us  [exchange(): lax.ppermute(pieces[k], 'hid', [(i, (i + k) % parts) for i in range(parts)])]
    pallas_call x2 -> x3, Pallas kernels: 8.34 us -> 19.4 us  [the longest x2 12.7 us: unit_sums(): pl.pallas_call(functools.partial(sum_kernel, height), grid_spec=pltpu.Pre...]
    all_to_all x3, starting transfers between devices: 17.1 us -> 21.3 us  [swap(): return lax.all_to_all(array, 'dom', split_axis=0, concat_axis=0, tiled=True)]
    select_n x1 -> x0, other arithmetic: 4.16 us -> none  [local(): grad = jnp.where(pre_relu > 0, grad_out, jnp.zeros_like(grad_out))]
  transfers between devices with their start and end apart: 13 -> 13, of which waited for: 4 -> 6; matrix products, arithmetic and copies ran while one was open for 1% -> 2% of each run, Pallas kernels for 11% -> 12%
where the time goes in v2:
time: 274 us; the launch traced here: 273 us
  blocking collectives  118 us (43%)
  Pallas kernels  54.2 us (20%)
  waiting for transfers between devices  37.8 us (14%)
  starting transfers between devices  36.3 us (13%)
  between operations  14.2 us (5%)
  local copies, waits for them, and re-layouts  8.62 us (3%)
  other arithmetic  3.7 us (1%)
    all_to_all x1, blocking collectives, swap(): return lax.all_to_all(array, 'dom', split_axis=0, concat_axis=0, tiled=True)  118 us
    all_to_all x3, waiting for transfers between devices, swap(): return lax.all_to_all(array, 'dom', split_axis=0, concat_axis=0, tiled=True)  32.5 us
    all_to_all x3, starting transfers between devices, swap(): return lax.all_to_all(array, 'dom', split_axis=0, concat_axis=0, tiled=True)  21.3 us
    pallas_call x1, Pallas kernels, messages(): pl.pallas_call(message_kernel, grid_spec=pltpu.PrefetchScalarGridSpec(num...  15.6 us
    ppermute x9, starting transfers between devices, exchange(): lax.ppermute(pieces[k], 'hid', [(i, (i + k) % parts) for i in range(parts)])  14.9 us
    pallas_call x2, Pallas kernels, unit_sums(): pl.pallas_call(functools.partial(sum_kernel, height), grid_spec=pltpu.Pre...  12.7 us
    pallas_call x1, Pallas kernels, weight_parts(): pl.pallas_call(weight_kernel, grid_spec=pltpu.PrefetchScalarGridSpec(num_...  10 us
    pallas_call x1, Pallas kernels, turn(): pl.pallas_call(turn_kernel, grid_spec=pltpu.PrefetchScalarGridSpec(num_sc...  7.04 us
  transfers between devices with their start and end apart: 13, of which 6 were waited for; matrix products, arithmetic and copies ran while one was open for 2% of the time, Pallas kernels for 12%

profile of v2, /device:TPU:1, one launch (start us, length us, event | category | flops | bytes accessed | tf_op | source)
XLA Modules:
  0.0 273.2 jit_solution(6052438271021231149)
XLA Ops:
  7.2 0.0 all-gather.2.cloned.1.call-start
  7.2 6.7 %masked.1.far_grad = bf16[13312,128]{1,0:T(8,128)(2,1)} custom-call(bf16[12288,128]{1,0:T(8,128)(2,1)} %pre_relu.1, bf16[12288,128]{1,0:T(8,128)(2,1)} %grad_out.1, bf16[128,512]{1,0:T(8,128)(2,1)} %near.1, bf16[128,512]{1,0:T(8,128)(2,1)} %own.1), custom_call_target="tpu_custom_call" | custom-call | bytes 9437 | tf_op jit(solution)/shard_map/masked/pallas_call | solution.py:59
  13.9 0.0 copy-start.5
  13.9 0.0 copy-start.6
  13.9 0.0 copy-start.7
  13.9 0.0 all-gather.2.cloned.1.call-update
  13.9 0.6 copy-done.5
  14.6 0.2 convert_reduce_fusion
  14.8 0.0 copy-done.6
  14.8 0.0 copy-done.7
  14.8 0.8 select_reduce_fusion
  15.6 0.1 convert_element_type.21
  15.7 0.7 pad.4.cols
  16.4 15.6 %messages.1 = (bf16[32,1168,128]{2,1,0:T(8,128)(2,1)}, bf16[32,384,128]{2,1,0:T(8,128)(2,1)}) custom-call(s32[384]{0:T(512)} %get-tuple-element.94.tile_ids, s32[384]{0:T(512)} %get-tuple-element.93.row_ids, bf16[13312,128]{1,0:T(8,128)(2,1)} %masked.1.far_grad, s32[1,12288]{1,0:T(1,128)} %bitcast.11, bf16[192,128,128]{2,1,0:T(8,128)(2,1)} %far_tiles.1, ...), custom_call_target="tpu_custom_call" | custom-call | flops 1610612 | bytes 22020 | tf_op jit(solution)/shard_map/messages/pallas_call | solution.py:127
  32.0 118.4 %all_to_all.20.received = bf16[32,1168,128]{2,1,0:T(8,128)(2,1)} all-to-all(bf16[32,1168,128]{2,1,0:T(8,128)(2,1)} %get-tuple-element.51), channel_id=1, replica_groups=mesh['dom'=32,'hid'=4] {'dom'}, dimensions={0} | all-to-all | bytes 19136512 | tf_op jit(solution)/shard_map/all_to_all | solution.py:376
  150.4 4.6 %all-to-all-start.1 = ((bf16[32,384,128]{2,1,0:T(8,128)(2,1)}), bf16[32,384,128]{2,1,0:T(8,128)(2,1)S(1)}, u32[]{:S(2)}, u32[]{:S(2)}) async-start(bf16[32,384,128]{2,1,0:T(8,128)(2,1)} %get-tuple-element.53), calls=%async_computation.1 | async-start | bytes 6291456 | tf_op jit(solution)/shard_map/all_to_all | solution.py:376
  155.0 8.4 %unit_sums.2 = (bf16[96,3072]{1,0:T(8,128)(2,1)S(1)}, bf16[96,3072]{1,0:T(8,128)(2,1)}, bf16[96,3072]{1,0:T(8,128)(2,1)}, bf16[96,3072]{1,0:T(8,128)(2,1)}, s32[32,128]{1,0:T(8,128)S(1)}) custom-call(s32[1]{0:T(128)} %bitcast.2.place, bf16[32,1168,128]{2,1,0:T(8,128)(2,1)} %all_to_all.20.received), custom_call_target="tpu_custom_call" | custom-call | flops 4718 | bytes 9437 | tf_op jit(solution)/shard_map/unit_sums/pallas_call | solution.py:211
  163.4 0.0 copy-start.2
  163.4 0.8 copy-done.2
  164.2 0.0 all-gather.2.cloned.1.call-done.grad.rest_8_.rest_9_
  164.2 1.3 collective-permute-start
  165.5 2.6 collective-permute-start.1
  168.1 1.1 collective-permute-start.2
  169.2 0.0 copy-start
  169.2 1.9 copy-done
  171.1 0.0 copy-start.1
  171.1 1.9 copy-done.1
  172.9 10.0 %weight_parts.1 = f32[32,40,128]{2,1,0:T(8,128)} custom-call(s32[1]{0:T(128)} %bitcast.2.place, bf16[12288,128]{1,0:T(8,128)(2,1)S(1)} %copy-done, bf16[12288,128]{1,0:T(8,128)(2,1)S(1)} %copy-done.1, bf16[13312,512]{1,0:T(8,128)(2,1)} %all-gather.2.cloned.1.call-done.grad.rest_8_.rest_9_), custom_call_target="tpu_custom_call" | custom-call | flops 3221225 | bytes 19922 | tf_op jit(solution)/shard_map/weight_parts/pallas_call | solution.py:323
  183.0 11.2 %all-to-all-done.1.received = bf16[32,384,128]{2,1,0:T(8,128)(2,1)S(1)} async-done(((bf16[32,384,128]{2,1,0:T(8,128)(2,1)}), bf16[32,384,128]{2,1,0:T(8,128)(2,1)S(1)}, u32[]{:S(2)}, u32[]{:S(2)}) %all-to-all-start.1) | async-done | bytes 3145760 | tf_op jit(solution)/shard_map/all_to_all | solution.py:376
  194.1 0.0 copy-start.3
  194.1 0.0 collective-permute-done.rest_1_
  194.2 0.2 collective-permute-done.1.rest_2_
  194.3 0.0 collective-permute-done.2.rest_3_
  194.3 4.3 %unit_sums.3 = (bf16[32,3072]{1,0:T(8,128)(2,1)S(1)}, bf16[32,3072]{1,0:T(8,128)(2,1)S(1)}, bf16[32,3072]{1,0:T(8,128)(2,1)S(1)}, bf16[32,3072]{1,0:T(8,128)(2,1)S(1)}) custom-call(s32[1]{0:T(128)} %bitcast.2.place, bf16[32,384,128]{2,1,0:T(8,128)(2,1)S(1)} %all-to-all-done.1.received, s32[32,128]{1,0:T(8,128)S(1)} %get-tuple-element.70.rest_0_), custom_call_target="tpu_custom_call" | custom-call | flops 1572 | bytes 9437 | tf_op jit(solution)/shard_map/unit_sums/pallas_call | solution.py:211
  198.7 1.2 collective-permute-start.3
  199.9 2.6 collective-permute-start.4
  202.5 1.1 collective-permute-start.5
  203.6 0.9 collective-permute-done.3.rest_5_
  204.5 4.2 %collective-permute-done.4.rest_6_ = bf16[32,3072]{1,0:T(8,128)(2,1)S(1)} collective-permute-done((bf16[32,3072]{1,0:T(8,128)(2,1)S(1)}, bf16[32,3072]{1,0:T(8,128)(2,1)S(1)}, u32[]{:S(2)}, u32[]{:S(2)}) %collective-permute-start.4) | collective-permute-done | bytes 196640 | tf_op jit(solution)/shard_map/ppermute | solution.py:371
  208.7 0.0 collective-permute-done.5.rest_7_
  208.7 0.0 copy-done.3
  208.7 7.0 %turn.1 = (bf16[3072,128]{1,0:T(8,128)(2,1)S(1)}, bf16[3072,128]{1,0:T(8,128)(2,1)}, bf16[3072,128]{1,0:T(8,128)(2,1)}, bf16[3072,128]{1,0:T(8,128)(2,1)S(1)}) custom-call(s32[1]{0:T(128)} %bitcast.2.place, bf16[96,3072]{1,0:T(8,128)(2,1)S(1)} %copy-done.3, bf16[96,3072]{1,0:T(8,128)(2,1)} %collective-permute-done.rest_1_, ...), custom_call_target="tpu_custom_call" | custom-call | flops 3221225 | bytes 10485 | tf_op jit(solution)/shard_map/turn/pallas_call | solution.py:272
  215.7 0.0 copy-start.4
  215.7 0.9 copy-done.4
  216.6 2.3 collective-permute-start.7
  218.9 10.5 %all-to-all-start.2 = ((f32[32,40,128]{2,1,0:T(8,128)}), f32[32,40,128]{2,1,0:T(8,128)}, u32[]{:S(2)}, u32[]{:S(2)}) async-start(f32[32,40,128]{2,1,0:T(8,128)} %weight_parts.1), calls=%async_computation.2 | async-start | bytes 1310720 | tf_op jit(solution)/shard_map/all_to_all | solution.py:376
  229.4 1.0 collective-permute-start.6
  230.4 1.8 collective-permute-start.8
  232.2 10.2 %all-to-all-done.2 = f32[32,40,128]{2,1,0:T(8,128)} async-done(((f32[32,40,128]{2,1,0:T(8,128)}), f32[32,40,128]{2,1,0:T(8,128)}, u32[]{:S(2)}, u32[]{:S(2)}) %all-to-all-start.2) | async-done | bytes 655392 | tf_op jit(solution)/shard_map/all_to_all | solution.py:376
  242.4 1.1 reduce_sum.49
  243.6 0.0 collective-permute-done.7.rest_2_
  243.6 0.9 broadcast_in_dim.38
  244.4 6.2 %all-to-all-start.3 = ((f32[32,32,128]{2,1,0:T(8,128)}), f32[32,32,128]{2,1,0:T(8,128)}, u32[]{:S(2)}, u32[]{:S(2)}) async-start(f32[32,32,128]{2,1,0:T(8,128)} %broadcast_in_dim.38), calls=%async_computation.3 | async-start | bytes 1048576 | tf_op jit(solution)/shard_map/all_to_all | solution.py:376
  250.7 0.5 multiply_bitcast_fusion.1
  251.2 11.1 %all-to-all-done.3 = f32[32,32,128]{2,1,0:T(8,128)} async-done(((f32[32,32,128]{2,1,0:T(8,128)}), f32[32,32,128]{2,1,0:T(8,128)}, u32[]{:S(2)}, u32[]{:S(2)}) %all-to-all-start.3) | async-done | bytes 524320 | tf_op jit(solution)/shard_map/all_to_all | solution.py:376
  262.3 1.1 multiply_bitcast_fusion
  263.4 0.0 collective-permute-done.6.rest_1_
  263.4 0.0 collective-permute-done.8.rest_3_
  263.4 0.8 fusion.1
  264.2 2.1 place_quarters.1
  (3 shorter events, 0.0 us)
Async XLA Ops:
  7.2 157.0 %all-gather.2.cloned.1.call-start = ((), (), s32[]{:S(2)}) async-start(), calls=%async_computation.4 | async-start | bytes 17039360 | tf_op jit(solution)/shard_map/all_gather | solution.py:403
  13.9 0.7 copy-start.5
  13.9 0.9 copy-start.6
  13.9 0.9 copy-start.7
  150.4 43.8 %all-to-all-start.1 = ((bf16[32,384,128]{2,1,0:T(8,128)(2,1)}), bf16[32,384,128]{2,1,0:T(8,128)(2,1)S(1)}, u32[]{:S(2)}, u32[]{:S(2)}) async-start(bf16[32,384,128]{2,1,0:T(8,128)(2,1)} %get-tuple-element.53), calls=%async_computation.1 | async-start | bytes 6291456 | tf_op jit(solution)/shard_map/all_to_all | solution.py:376
  163.4 0.8 copy-start.2
  164.2 30.0 %collective-permute-start = (bf16[96,3072]{1,0:T(8,128)(2,1)}, bf16[96,3072]{1,0:T(8,128)(2,1)}, u32[]{:S(2)}, u32[]{:S(2)}) collective-permute-start(bf16[96,3072]{1,0:T(8,128)(2,1)} %get-tuple-element.61), channel_id=1, source_target_pairs={{0,1},{1,2},{2,3},{3,0},{4,5},{5,6},{6,7},{7,4},{8,9},{9,10},{10,1... | collective-permute-start | bytes 1769480 | tf_op jit(solution)/shard_map/ppermute | solution.py:371
  165.5 28.8 %collective-permute-start.1 = (bf16[96,3072]{1,0:T(8,128)(2,1)}, bf16[96,3072]{1,0:T(8,128)(2,1)}, u32[]{:S(2)}, u32[]{:S(2)}) collective-permute-start(bf16[96,3072]{1,0:T(8,128)(2,1)} %get-tuple-element.62), channel_id=1, source_target_pairs={{0,2},{1,3},{2,0},{3,1},{4,6},{5,7},{6,4},{7,5},{8,10},{9,11},{10,... | collective-permute-start | bytes 1769480 | tf_op jit(solution)/shard_map/ppermute | solution.py:371
  168.1 26.2 %collective-permute-start.2 = (bf16[96,3072]{1,0:T(8,128)(2,1)}, bf16[96,3072]{1,0:T(8,128)(2,1)}, u32[]{:S(2)}, u32[]{:S(2)}) collective-permute-start(bf16[96,3072]{1,0:T(8,128)(2,1)} %get-tuple-element.63), channel_id=1, source_target_pairs={{0,3},{1,0},{2,1},{3,2},{4,7},{5,4},{6,5},{7,6},{8,11},{9,8},{10,9... | collective-permute-start | bytes 1769480 | tf_op jit(solution)/shard_map/ppermute | solution.py:371
  169.2 1.9 copy-start
  171.1 1.9 copy-start.1
  194.1 14.6 %copy-start.3 = (bf16[96,3072]{1,0:T(8,128)(2,1)S(1)}, bf16[96,3072]{1,0:T(8,128)(2,1)}, u32[]{:S(2)}) copy-start(bf16[96,3072]{1,0:T(8,128)(2,1)} %copy-done.2) | copy-start | bytes 1769476
  198.7 5.8 %collective-permute-start.3 = (bf16[32,3072]{1,0:T(8,128)(2,1)S(1)}, bf16[32,3072]{1,0:T(8,128)(2,1)S(1)}, u32[]{:S(2)}, u32[]{:S(2)}) collective-permute-start(bf16[32,3072]{1,0:T(8,128)(2,1)S(1)} %get-tuple-element.72), channel_id=1, source_target_pairs={{0,1},{1,2},{2,3},{3,0},{4,5},{5,6},{6,7},{7,4},{8,9},{9,10},{10,1... | collective-permute-start | bytes 589832 | tf_op jit(solution)/shard_map/ppermute | solution.py:371
  199.9 8.8 %collective-permute-start.4 = (bf16[32,3072]{1,0:T(8,128)(2,1)S(1)}, bf16[32,3072]{1,0:T(8,128)(2,1)S(1)}, u32[]{:S(2)}, u32[]{:S(2)}) collective-permute-start(bf16[32,3072]{1,0:T(8,128)(2,1)S(1)} %get-tuple-element.73), channel_id=1, source_target_pairs={{0,2},{1,3},{2,0},{3,1},{4,6},{5,7},{6,4},{7,5},{8,10},{9,11},{10,... | collective-permute-start | bytes 589832 | tf_op jit(solution)/shard_map/ppermute | solution.py:371
  202.5 6.2 %collective-permute-start.5 = (bf16[32,3072]{1,0:T(8,128)(2,1)S(1)}, bf16[32,3072]{1,0:T(8,128)(2,1)S(1)}, u32[]{:S(2)}, u32[]{:S(2)}) collective-permute-start(bf16[32,3072]{1,0:T(8,128)(2,1)S(1)} %get-tuple-element.74), channel_id=1, source_target_pairs={{0,3},{1,0},{2,1},{3,2},{4,7},{5,4},{6,5},{7,6},{8,11},{9,8},{10,9... | collective-permute-start | bytes 589832 | tf_op jit(solution)/shard_map/ppermute | solution.py:371
  215.7 0.9 copy-start.4
  216.6 26.9 %collective-permute-start.7 = (bf16[3072,128]{1,0:T(8,128)(2,1)}, bf16[3072,128]{1,0:T(8,128)(2,1)S(1)}, u32[]{:S(2)}, u32[]{:S(2)}) collective-permute-start(bf16[3072,128]{1,0:T(8,128)(2,1)} %get-tuple-element.82), channel_id=1, source_target_pairs={{0,2},{1,3},{2,0},{3,1},{4,6},{5,7},{6,4},{7,5},{8,10},{9,11},{10,... | collective-permute-start | bytes 2359304 | tf_op jit(solution)/shard_map/ppermute | solution.py:371
  218.9 23.5 %all-to-all-start.2 = ((f32[32,40,128]{2,1,0:T(8,128)}), f32[32,40,128]{2,1,0:T(8,128)}, u32[]{:S(2)}, u32[]{:S(2)}) async-start(f32[32,40,128]{2,1,0:T(8,128)} %weight_parts.1), calls=%async_computation.2 | async-start | bytes 1310720 | tf_op jit(solution)/shard_map/all_to_all | solution.py:376
  229.4 33.9 %collective-permute-start.6 = (bf16[3072,128]{1,0:T(8,128)(2,1)}, bf16[3072,128]{1,0:T(8,128)(2,1)S(1)}, u32[]{:S(2)}, u32[]{:S(2)}) collective-permute-start(bf16[3072,128]{1,0:T(8,128)(2,1)} %get-tuple-element.80), channel_id=1, source_target_pairs={{0,1},{1,2},{2,3},{3,0},{4,5},{5,6},{6,7},{7,4},{8,9},{9,10},{10,1... | collective-permute-start | bytes 2359304 | tf_op jit(solution)/shard_map/ppermute | solution.py:371
  230.4 32.9 %collective-permute-start.8 = (bf16[3072,128]{1,0:T(8,128)(2,1)}, bf16[3072,128]{1,0:T(8,128)(2,1)S(1)}, u32[]{:S(2)}, u32[]{:S(2)}) collective-permute-start(bf16[3072,128]{1,0:T(8,128)(2,1)} %copy-done.4), channel_id=1, source_target_pairs={{0,3},{1,0},{2,1},{3,2},{4,7},{5,4},{6,5},{7,6},{8,11},{9,8},{10,9... | collective-permute-start | bytes 2359304 | tf_op jit(solution)/shard_map/ppermute | solution.py:371
  244.4 17.8 %all-to-all-start.3 = ((f32[32,32,128]{2,1,0:T(8,128)}), f32[32,32,128]{2,1,0:T(8,128)}, u32[]{:S(2)}, u32[]{:S(2)}) async-start(f32[32,32,128]{2,1,0:T(8,128)} %broadcast_in_dim.38), calls=%async_computation.3 | async-start | bytes 1048576 | tf_op jit(solution)/shard_map/all_to_all | solution.py:376
Sparse Core Ops, SparseCore 0:
  14.0 134.1 all-gather.1

commit v3 on v2

--- a/solution.py
+++ b/solution.py
@@ -52,7 +52,7 @@
 def masked(pre_relu, grad_out, near, own):
     hosts = grad_out.shape[0]
     extra = 2 * near.shape[1]
-    chunk = 2 * extra
+    chunk = 4 * extra
     steps = hosts // chunk
     whole = pl.BlockSpec(memory_space=pltpu.VMEM)
     piece = pl.BlockSpec((chunk, BLK), lambda i: (jnp.minimum(i, steps - 1), 0))
@@ -249,18 +249,21 @@
             for i in range(parts):
                 sender = lax.rem(place[0] + parts - i, parts) * BLK
                 part = slice(i * BLK, (i + 1) * BLK)
-                near[here, part] = weights[lanes(sender, BLK), to]
+                near[part, here] = weights[lanes(sender, BLK), to].T
                 own[part, here] = weights[units + i * BLK : units + (i + 1) * BLK, to].T
 
     at = lanes(step * chunk, chunk)
     sums = []
     for head, tail in zip(heads, tails):
         sums += [head[:, at], tail[:, at]]
-    turned = jnp.dot(near[...], jnp.concatenate(sums, axis=0), preferred_element_type=F32)
-    result = jnp.dot(grad[...], own[...], preferred_element_type=F32)
+    result = jnp.dot(grad[...], own[...], preferred_element_type=F32) + lax.dot_general(
+        jnp.concatenate(sums, axis=0),
+        near[...],
+        (((0,), (0,)), ((), ())),
+        preferred_element_type=F32,
+    )
     for k, out in enumerate(outs):
-        part = result[:, k * BLK : (k + 1) * BLK] + turned[k * BLK : (k + 1) * BLK, :].T
-        out[...] = part.astype(BF16)
+        out[...] = result[:, k * BLK : (k + 1) * BLK].astype(BF16)
 
 
 def turn(place, heads, tails, grad):
@@ -424,8 +427,9 @@
     pieces = weight_parts(place, features, neigh_mean, full_grad, owners)
     tail, pieces, heads = lax.optimization_barrier((tail, pieces, heads))
     tails = unit_sums(TAIL, place, tail, blocks, parts, marks)
-    quarters = turn(place, heads, exchange(tails), full_grad)
-    pieces, quarters = lax.optimization_barrier((pieces, quarters))
+    tails = exchange(tails)
+    tails[2], pieces = lax.optimization_barrier((tails[2], pieces))
+    quarters = turn(place, heads, tails, full_grad)
     quarters = exchange(quarters)
     summed = jnp.sum(swap(pieces), axis=0)
     rows = 8 * parts

time: 274 us -> 272 us (level)
    all_to_all x3, starting transfers between devices: 21.3 us -> 18.5 us  [swap(): return lax.all_to_all(array, 'dom', split_axis=0, concat_axis=0, tiled=True)]
  transfers between devices with their start and end apart: 13 -> 13, of which waited for: 6 -> 6; matrix products, arithmetic and copies ran while one was open for 2% -> 2% of each run, Pallas kernels for 12% -> 13%
where the time goes in v3:
time: 272 us; the launch traced here: 271 us
  blocking collectives  118 us (43%)
  Pallas kernels  53.8 us (20%)
  waiting for transfers between devices  38.4 us (14%)
  starting transfers between devices  34.2 us (13%)
  between operations  14.2 us (5%)
  local copies, waits for them, and re-layouts  8.62 us (3%)
  other arithmetic  3.7 us (1%)
    all_to_all x1, blocking collectives, swap(): return lax.all_to_all(array, 'dom', split_axis=0, concat_axis=0, tiled=True)  118 us
    all_to_all x3, waiting for transfers between devices, swap(): return lax.all_to_all(array, 'dom', split_axis=0, concat_axis=0, tiled=True)  32.3 us
    all_to_all x3, starting transfers between devices, swap(): return lax.all_to_all(array, 'dom', split_axis=0, concat_axis=0, tiled=True)  18.5 us
    ppermute x9, starting transfers between devices, exchange(): lax.ppermute(pieces[k], 'hid', [(i, (i + k) % parts) for i in range(parts)])  15.6 us
    pallas_call x1, Pallas kernels, messages(): pl.pallas_call(message_kernel, grid_spec=pltpu.PrefetchScalarGridSpec(num...  15.6 us
    pallas_call x2, Pallas kernels, unit_sums(): pl.pallas_call(functools.partial(sum_kernel, height), grid_spec=pltpu.Pre...  12.9 us
    pallas_call x1, Pallas kernels, weight_parts(): pl.pallas_call(weight_kernel, grid_spec=pltpu.PrefetchScalarGridSpec(num_...  10 us
    pallas_call x1, Pallas kernels, turn(): pl.pallas_call(turn_kernel, grid_spec=pltpu.PrefetchScalarGridSpec(num_sc...  7.22 us
  transfers between devices with their start and end apart: 13, of which 6 were waited for; matrix products, arithmetic and copies ran while one was open for 2% of the time, Pallas kernels for 13%

profile of v3, /device:TPU:1, one launch (start us, length us, event | category | flops | bytes accessed | tf_op | source)
XLA Modules:
  0.0 271.4 jit_solution(5364974316131476352)
XLA Ops:
  7.2 0.0 all-gather.2.cloned.1.call-start
  7.2 5.8 %masked.1.far_grad = bf16[13312,128]{1,0:T(8,128)(2,1)} custom-call(bf16[12288,128]{1,0:T(8,128)(2,1)} %pre_relu.1, bf16[12288,128]{1,0:T(8,128)(2,1)} %grad_out.1, bf16[128,512]{1,0:T(8,128)(2,1)} %near.1, bf16[128,512]{1,0:T(8,128)(2,1)} %own.1), custom_call_target="tpu_custom_call" | custom-call | bytes 9437 | tf_op jit(solution)/shard_map/masked/pallas_call | solution.py:59
  13.1 0.0 copy-start.5
  13.1 0.0 copy-start.6
  13.1 0.0 copy-start.7
  13.1 0.0 all-gather.2.cloned.1.call-update
  13.1 0.6 copy-done.5
  13.7 0.2 convert_reduce_fusion
  13.9 0.0 copy-done.6
  13.9 0.0 copy-done.7
  14.0 0.8 select_reduce_fusion
  14.7 0.1 convert_element_type.21
  14.8 0.7 pad.4.cols
  15.5 15.6 %messages.1 = (bf16[32,1168,128]{2,1,0:T(8,128)(2,1)}, bf16[32,384,128]{2,1,0:T(8,128)(2,1)}) custom-call(s32[384]{0:T(512)} %get-tuple-element.88.tile_ids, s32[384]{0:T(512)} %get-tuple-element.87.row_ids, bf16[13312,128]{1,0:T(8,128)(2,1)} %masked.1.far_grad, s32[1,12288]{1,0:T(1,128)} %bitcast.11, bf16[192,128,128]{2,1,0:T(8,128)(2,1)} %far_tiles.1, ...), custom_call_target="tpu_custom_call" | custom-call | flops 1610612 | bytes 22020 | tf_op jit(solution)/shard_map/messages/pallas_call | solution.py:127
  31.1 118.5 %all_to_all.20.received = bf16[32,1168,128]{2,1,0:T(8,128)(2,1)} all-to-all(bf16[32,1168,128]{2,1,0:T(8,128)(2,1)} %get-tuple-element.48), channel_id=1, replica_groups=mesh['dom'=32,'hid'=4] {'dom'}, dimensions={0} | all-to-all | bytes 19136512 | tf_op jit(solution)/shard_map/all_to_all | solution.py:379
  149.6 4.6 %all-to-all-start.1 = ((bf16[32,384,128]{2,1,0:T(8,128)(2,1)}), bf16[32,384,128]{2,1,0:T(8,128)(2,1)S(1)}, u32[]{:S(2)}, u32[]{:S(2)}) async-start(bf16[32,384,128]{2,1,0:T(8,128)(2,1)} %get-tuple-element.50), calls=%async_computation.1 | async-start | bytes 6291456 | tf_op jit(solution)/shard_map/all_to_all | solution.py:379
  154.2 8.5 %unit_sums.2 = (bf16[96,3072]{1,0:T(8,128)(2,1)S(1)}, bf16[96,3072]{1,0:T(8,128)(2,1)}, bf16[96,3072]{1,0:T(8,128)(2,1)}, bf16[96,3072]{1,0:T(8,128)(2,1)}, s32[32,128]{1,0:T(8,128)S(1)}) custom-call(s32[1]{0:T(128)} %bitcast.2.place, bf16[32,1168,128]{2,1,0:T(8,128)(2,1)} %all_to_all.20.received), custom_call_target="tpu_custom_call" | custom-call | flops 4718 | bytes 9437 | tf_op jit(solution)/shard_map/unit_sums/pallas_call | solution.py:211
  162.7 0.0 copy-start.2
  162.7 0.8 copy-done.2
  163.5 0.0 all-gather.2.cloned.1.call-done.grad.rest_8_.rest_9_
  163.5 1.3 collective-permute-start
  164.8 2.7 collective-permute-start.1
  167.4 1.1 collective-permute-start.2
  168.5 0.0 copy-start
  168.5 1.9 copy-done
  170.4 0.0 copy-start.1
  170.4 1.9 copy-done.1
  172.3 10.0 %weight_parts.1 = f32[32,40,128]{2,1,0:T(8,128)} custom-call(s32[1]{0:T(128)} %bitcast.2.place, bf16[12288,128]{1,0:T(8,128)(2,1)S(1)} %copy-done, bf16[12288,128]{1,0:T(8,128)(2,1)S(1)} %copy-done.1, bf16[13312,512]{1,0:T(8,128)(2,1)} %all-gather.2.cloned.1.call-done.grad.rest_8_.rest_9_), custom_call_target="tpu_custom_call" | custom-call | flops 3221225 | bytes 19922 | tf_op jit(solution)/shard_map/weight_parts/pallas_call | solution.py:326
  182.3 11.0 %all-to-all-done.1.received = bf16[32,384,128]{2,1,0:T(8,128)(2,1)S(1)} async-done(((bf16[32,384,128]{2,1,0:T(8,128)(2,1)}), bf16[32,384,128]{2,1,0:T(8,128)(2,1)S(1)}, u32[]{:S(2)}, u32[]{:S(2)}) %all-to-all-start.1) | async-done | bytes 3145760 | tf_op jit(solution)/shard_map/all_to_all | solution.py:379
  193.4 0.0 copy-start.3
  193.4 0.0 collective-permute-done.rest_1_
  193.4 0.4 collective-permute-done.1.rest_2_
  193.8 0.0 collective-permute-done.2.rest_3_
  193.8 4.5 %unit_sums.3 = (bf16[32,3072]{1,0:T(8,128)(2,1)S(1)}, bf16[32,3072]{1,0:T(8,128)(2,1)S(1)}, bf16[32,3072]{1,0:T(8,128)(2,1)S(1)}, bf16[32,3072]{1,0:T(8,128)(2,1)S(1)}) custom-call(s32[1]{0:T(128)} %bitcast.2.place, bf16[32,384,128]{2,1,0:T(8,128)(2,1)S(1)} %all-to-all-done.1.received, s32[32,128]{1,0:T(8,128)S(1)} %get-tuple-element.66.rest_0_), custom_call_target="tpu_custom_call" | custom-call | flops 1572 | bytes 9437 | tf_op jit(solution)/shard_map/unit_sums/pallas_call | solution.py:211
  198.3 2.6 collective-permute-start.4
  200.9 0.4 collective-permute-start.3
  201.3 2.3 collective-permute-start.5
  203.6 0.8 collective-permute-done.4.rest_6_
  204.4 4.8 %collective-permute-done.3.rest_5_ = bf16[32,3072]{1,0:T(8,128)(2,1)S(1)} collective-permute-done((bf16[32,3072]{1,0:T(8,128)(2,1)S(1)}, bf16[32,3072]{1,0:T(8,128)(2,1)S(1)}, u32[]{:S(2)}, u32[]{:S(2)}) %collective-permute-start.3) | collective-permute-done | bytes 196640 | tf_op jit(solution)/shard_map/ppermute | solution.py:374
  209.2 0.0 collective-permute-done.5.rest_7_
  209.2 0.0 copy-done.3
  209.2 7.2 %turn.1 = (bf16[3072,128]{1,0:T(8,128)(2,1)S(1)}, bf16[3072,128]{1,0:T(8,128)(2,1)}, bf16[3072,128]{1,0:T(8,128)(2,1)}, bf16[3072,128]{1,0:T(8,128)(2,1)S(1)}) custom-call(s32[1]{0:T(128)} %bitcast.2.place, bf16[96,3072]{1,0:T(8,128)(2,1)S(1)} %copy-done.3, bf16[96,3072]{1,0:T(8,128)(2,1)} %collective-permute-done.rest_1_, ...), custom_call_target="tpu_custom_call" | custom-call | flops 3221225 | bytes 10485 | tf_op jit(solution)/shard_map/turn/pallas_call | solution.py:275
  216.4 0.0 copy-start.4
  216.4 0.9 copy-done.4
  217.3 2.6 collective-permute-start.7
  219.9 7.9 %all-to-all-start.2 = ((f32[32,40,128]{2,1,0:T(8,128)}), f32[32,40,128]{2,1,0:T(8,128)}, u32[]{:S(2)}, u32[]{:S(2)}) async-start(f32[32,40,128]{2,1,0:T(8,128)} %weight_parts.1), calls=%async_computation.2 | async-start | bytes 1310720 | tf_op jit(solution)/shard_map/all_to_all | solution.py:379
  227.8 1.2 collective-permute-start.6
  229.0 1.5 collective-permute-start.8
  230.5 10.2 %all-to-all-done.2 = f32[32,40,128]{2,1,0:T(8,128)} async-done(((f32[32,40,128]{2,1,0:T(8,128)}), f32[32,40,128]{2,1,0:T(8,128)}, u32[]{:S(2)}, u32[]{:S(2)}) %all-to-all-start.2) | async-done | bytes 655392 | tf_op jit(solution)/shard_map/all_to_all | solution.py:379
  240.7 1.1 reduce_sum.49
  241.9 0.0 collective-permute-done.7.rest_2_
  241.9 0.9 broadcast_in_dim.38
  242.8 6.0 %all-to-all-start.3 = ((f32[32,32,128]{2,1,0:T(8,128)}), f32[32,32,128]{2,1,0:T(8,128)}, u32[]{:S(2)}, u32[]{:S(2)}) async-start(f32[32,32,128]{2,1,0:T(8,128)} %broadcast_in_dim.38), calls=%async_computation.3 | async-start | bytes 1048576 | tf_op jit(solution)/shard_map/all_to_all | solution.py:379
  248.8 0.5 multiply_bitcast_fusion.1
  249.3 11.1 %all-to-all-done.3 = f32[32,32,128]{2,1,0:T(8,128)} async-done(((f32[32,32,128]{2,1,0:T(8,128)}), f32[32,32,128]{2,1,0:T(8,128)}, u32[]{:S(2)}, u32[]{:S(2)}) %all-to-all-start.3) | async-done | bytes 524320 | tf_op jit(solution)/shard_map/all_to_all | solution.py:379
  260.4 1.1 multiply_bitcast_fusion
  261.5 0.0 collective-permute-done.6.rest_1_
  261.5 0.0 collective-permute-done.8.rest_3_
  261.5 0.8 fusion.1
  262.4 2.1 place_quarters.1
  (3 shorter events, 0.0 us)
Async XLA Ops:
  7.2 156.3 %all-gather.2.cloned.1.call-start = ((), (), s32[]{:S(2)}) async-start(), calls=%async_computation.4 | async-start | bytes 17039360 | tf_op jit(solution)/shard_map/all_gather | solution.py:406
  13.1 0.7 copy-start.5
  13.1 0.9 copy-start.6
  13.1 0.9 copy-start.7
  149.6 43.8 %all-to-all-start.1 = ((bf16[32,384,128]{2,1,0:T(8,128)(2,1)}), bf16[32,384,128]{2,1,0:T(8,128)(2,1)S(1)}, u32[]{:S(2)}, u32[]{:S(2)}) async-start(bf16[32,384,128]{2,1,0:T(8,128)(2,1)} %get-tuple-element.50), calls=%async_computation.1 | async-start | bytes 6291456 | tf_op jit(solution)/shard_map/all_to_all | solution.py:379
  162.7 0.8 copy-start.2
  163.5 29.9 %collective-permute-start = (bf16[96,3072]{1,0:T(8,128)(2,1)}, bf16[96,3072]{1,0:T(8,128)(2,1)}, u32[]{:S(2)}, u32[]{:S(2)}) collective-permute-start(bf16[96,3072]{1,0:T(8,128)(2,1)} %get-tuple-element.58), channel_id=1, source_target_pairs={{0,1},{1,2},{2,3},{3,0},{4,5},{5,6},{6,7},{7,4},{8,9},{9,10},{10,1... | collective-permute-start | bytes 1769480 | tf_op jit(solution)/shard_map/ppermute | solution.py:374
  164.8 29.0 %collective-permute-start.1 = (bf16[96,3072]{1,0:T(8,128)(2,1)}, bf16[96,3072]{1,0:T(8,128)(2,1)}, u32[]{:S(2)}, u32[]{:S(2)}) collective-permute-start(bf16[96,3072]{1,0:T(8,128)(2,1)} %get-tuple-element.59), channel_id=1, source_target_pairs={{0,2},{1,3},{2,0},{3,1},{4,6},{5,7},{6,4},{7,5},{8,10},{9,11},{10,... | collective-permute-start | bytes 1769480 | tf_op jit(solution)/shard_map/ppermute | solution.py:374
  167.4 26.4 %collective-permute-start.2 = (bf16[96,3072]{1,0:T(8,128)(2,1)}, bf16[96,3072]{1,0:T(8,128)(2,1)}, u32[]{:S(2)}, u32[]{:S(2)}) collective-permute-start(bf16[96,3072]{1,0:T(8,128)(2,1)} %get-tuple-element.60), channel_id=1, source_target_pairs={{0,3},{1,0},{2,1},{3,2},{4,7},{5,4},{6,5},{7,6},{8,11},{9,8},{10,9... | collective-permute-start | bytes 1769480 | tf_op jit(solution)/shard_map/ppermute | solution.py:374
  168.5 1.9 copy-start
  170.4 1.9 copy-start.1
  193.4 15.8 %copy-start.3 = (bf16[96,3072]{1,0:T(8,128)(2,1)S(1)}, bf16[96,3072]{1,0:T(8,128)(2,1)}, u32[]{:S(2)}) copy-start(bf16[96,3072]{1,0:T(8,128)(2,1)} %copy-done.2) | copy-start | bytes 1769476
  198.3 6.1 %collective-permute-start.4 = (bf16[32,3072]{1,0:T(8,128)(2,1)S(1)}, bf16[32,3072]{1,0:T(8,128)(2,1)S(1)}, u32[]{:S(2)}, u32[]{:S(2)}) collective-permute-start(bf16[32,3072]{1,0:T(8,128)(2,1)S(1)} %get-tuple-element.69), channel_id=1, source_target_pairs={{0,2},{1,3},{2,0},{3,1},{4,6},{5,7},{6,4},{7,5},{8,10},{9,11},{10,... | collective-permute-start | bytes 589832 | tf_op jit(solution)/shard_map/ppermute | solution.py:374
  200.9 8.3 %collective-permute-start.3 = (bf16[32,3072]{1,0:T(8,128)(2,1)S(1)}, bf16[32,3072]{1,0:T(8,128)(2,1)S(1)}, u32[]{:S(2)}, u32[]{:S(2)}) collective-permute-start(bf16[32,3072]{1,0:T(8,128)(2,1)S(1)} %get-tuple-element.68), channel_id=1, source_target_pairs={{0,1},{1,2},{2,3},{3,0},{4,5},{5,6},{6,7},{7,4},{8,9},{9,10},{10,1... | collective-permute-start | bytes 589832 | tf_op jit(solution)/shard_map/ppermute | solution.py:374
  201.3 7.9 %collective-permute-start.5 = (bf16[32,3072]{1,0:T(8,128)(2,1)S(1)}, bf16[32,3072]{1,0:T(8,128)(2,1)S(1)}, u32[]{:S(2)}, u32[]{:S(2)}) collective-permute-start(bf16[32,3072]{1,0:T(8,128)(2,1)S(1)} %get-tuple-element.72), channel_id=1, source_target_pairs={{0,3},{1,0},{2,1},{3,2},{4,7},{5,4},{6,5},{7,6},{8,11},{9,8},{10,9... | collective-permute-start | bytes 589832 | tf_op jit(solution)/shard_map/ppermute | solution.py:374
  216.4 0.9 copy-start.4
  217.3 24.6 %collective-permute-start.7 = (bf16[3072,128]{1,0:T(8,128)(2,1)}, bf16[3072,128]{1,0:T(8,128)(2,1)S(1)}, u32[]{:S(2)}, u32[]{:S(2)}) collective-permute-start(bf16[3072,128]{1,0:T(8,128)(2,1)} %get-tuple-element.76), channel_id=1, source_target_pairs={{0,2},{1,3},{2,0},{3,1},{4,6},{5,7},{6,4},{7,5},{8,10},{9,11},{10,... | collective-permute-start | bytes 2359304 | tf_op jit(solution)/shard_map/ppermute | solution.py:374
  219.9 20.8 %all-to-all-start.2 = ((f32[32,40,128]{2,1,0:T(8,128)}), f32[32,40,128]{2,1,0:T(8,128)}, u32[]{:S(2)}, u32[]{:S(2)}) async-start(f32[32,40,128]{2,1,0:T(8,128)} %weight_parts.1), calls=%async_computation.2 | async-start | bytes 1310720 | tf_op jit(solution)/shard_map/all_to_all | solution.py:379
  227.8 33.7 %collective-permute-start.6 = (bf16[3072,128]{1,0:T(8,128)(2,1)}, bf16[3072,128]{1,0:T(8,128)(2,1)S(1)}, u32[]{:S(2)}, u32[]{:S(2)}) collective-permute-start(bf16[3072,128]{1,0:T(8,128)(2,1)} %get-tuple-element.74), channel_id=1, source_target_pairs={{0,1},{1,2},{2,3},{3,0},{4,5},{5,6},{6,7},{7,4},{8,9},{9,10},{10,1... | collective-permute-start | bytes 2359304 | tf_op jit(solution)/shard_map/ppermute | solution.py:374
  229.0 32.5 %collective-permute-start.8 = (bf16[3072,128]{1,0:T(8,128)(2,1)}, bf16[3072,128]{1,0:T(8,128)(2,1)S(1)}, u32[]{:S(2)}, u32[]{:S(2)}) collective-permute-start(bf16[3072,128]{1,0:T(8,128)(2,1)} %copy-done.4), channel_id=1, source_target_pairs={{0,3},{1,0},{2,1},{3,2},{4,7},{5,4},{6,5},{7,6},{8,11},{9,8},{10,9... | collective-permute-start | bytes 2359304 | tf_op jit(solution)/shard_map/ppermute | solution.py:374
  242.8 17.7 %all-to-all-start.3 = ((f32[32,32,128]{2,1,0:T(8,128)}), f32[32,32,128]{2,1,0:T(8,128)}, u32[]{:S(2)}, u32[]{:S(2)}) async-start(f32[32,32,128]{2,1,0:T(8,128)} %broadcast_in_dim.38), calls=%async_computation.3 | async-start | bytes 1048576 | tf_op jit(solution)/shard_map/all_to_all | solution.py:379
Sparse Core Ops, SparseCore 0:
  13.2 134.1 all-gather.1
